TPU v7x, 32 devices: a whole 2x2x4 slice. The times are simulated.
32 devices in a mesh: batch: 4 (over z), ctx: 4 (over y, core), heads: 2 (over x).
Axes of the slice: x: 2, y: 2, z: 4, core: 2. Of those that a mesh axis runs over, the one named last changes fastest.
Arguments:
- tokens: bfloat16 [49152, 768], P(('batch', 'ctx', 'heads')), may hold values from -6 to 6
- lengths: int32 [4, 2], P('batch'), may hold values from 1536 to 10752, as said below
- gain_one: float32 [768], replicated, may hold values from 0.25 to 1.75
- w_qkv: bfloat16 [768, 3, 768], P(None, None, 'heads'), may hold values from -0.21875 to 0.21875
- f_query: bfloat16 [12, 64, 64], P('heads'), may hold values from -1.5 to 1.5
- f_key: bfloat16 [12, 64, 64], P('heads'), may hold values from -1.5 to 1.5
- w_out: bfloat16 [768, 768], P('heads'), may hold values from -3.5 to 3.5
- gain_two: float32 [768], replicated, may hold values from 0.25 to 1.75
- w_up: bfloat16 [768, 3072], P(None, 'heads'), may hold values from -0.21875 to 0.21875
- w_down: bfloat16 [3072, 768], P('heads'), may hold values from -0.109375 to 0.109375
- d_out: bfloat16 [49152, 768], P(('batch', 'ctx', 'heads')), may hold values from -6 to 6
Outputs:
- mixed: bfloat16 [49152, 768], P(('batch', 'ctx', 'heads'))
- grad_tokens: bfloat16 [49152, 768], P(('batch', 'ctx', 'heads'))
- grad_gain_one: float32 [768], replicated
- grad_w_qkv: float32 [768, 3, 768], P(None, None, 'heads')
- grad_f_query: float32 [12, 64, 64], P('heads')
- grad_f_key: float32 [12, 64, 64], P('heads')
- grad_w_out: float32 [768, 768], P('heads')
- grad_gain_two: float32 [768], replicated
- grad_w_up: float32 [768, 3072], P(None, 'heads')
- grad_w_down: float32 [3072, 768], P('heads')
Inputs may be any that keep to these rules, and one draw needn't show every extreme that they name: `lengths`: each row holds 1536 and 10752 in one of the two orders.
All inputs are finite; a program needn't handle non-finite values.
Results may differ from a plain program's by a relative error of at most 0.015.
Values may be sent and summed in bfloat16 or wider, within the bound.
No kernel may reach another device: no remote copies, remote signals or barrier semaphores. Data moves between devices by JAX's collectives and lax.ppermute only.
A program may use at most 448 MiB of HBM per device.

v0:
```python
import functools

import jax
import jax.numpy as jnp
import numpy as np
from jax import lax
from jax.experimental import pallas as pl
from jax.experimental.pallas import tpu as pltpu
from jax.sharding import PartitionSpec as P

epsilon = 1e-05
f32 = jnp.float32
bf16 = jnp.bfloat16
CHUNK = 256
BLOCK = 512
VMEM_LIMIT = 60 * 1024 * 1024
GELU_A = 0.7978845608028654
GELU_B = 0.044715


def dot(left, right):
    return lax.dot_general(left, right, (((1,), (0,)), ((), ())), preferred_element_type=f32)


def dot_t(left, right):
    return lax.dot_general(left, right, (((1,), (1,)), ((), ())), preferred_element_type=f32)


def params():
    return pltpu.CompilerParams(
        dimension_semantics=("arbitrary",), vmem_limit_bytes=VMEM_LIMIT
    )


def cost(micros):
    return pl.CostEstimate(flops=0, bytes_accessed=micros * 3_600_000, transcendentals=0)


def shaped(shape, kind=bf16):
    return jax.ShapeDtypeStruct(shape, kind)


def once(shape):
    zeros = (0,) * len(shape)
    return pl.BlockSpec(shape, lambda *_: zeros, pipeline_mode=pl.Buffered(1))


def by_rows(count, cols, at=0):
    return pl.BlockSpec((count, cols), lambda c, *_: (c, at))


def by_cols(rows, count, at=0):
    return pl.BlockSpec((rows, count), lambda c, *_: (at, c))


def map_block(maps, kind):
    return pl.BlockSpec(
        (1, *maps.shape[1:]), lambda *_: (kind, 0, 0, 0), pipeline_mode=pl.Buffered(1)
    )


anywhere = pl.BlockSpec(memory_space=pl.ANY)
scalars = pl.BlockSpec(memory_space=pltpu.SMEM)


def first_lanes():
    return lax.broadcasted_iota(jnp.int32, (1, 128), 1) < 64


def first_sublanes():
    return lax.broadcasted_iota(jnp.int32, (128, 1), 0) < 64


def build_maps(f, signs, turned_out, plain_out, pairs):
    top = first_sublanes()
    left = lax.broadcasted_iota(jnp.int32, (1, 256), 1) < 128
    for p in range(pairs):
        both = dot(f[0, 2 * p : 2 * p + 2].reshape(128, 64), signs[...])
        plain = jnp.where(top == left, both, 0.0)
        plain_out[p] = plain.astype(bf16)
        turned_out[p] = plain.T.astype(bf16)


def soft_rows(logits):
    count, size = logits.shape
    groups = logits.reshape(count // 64, 64, size)
    grown = jnp.exp(groups - jnp.max(groups, axis=1, keepdims=True))
    soft = grown * (1.0 / jnp.sum(grown, axis=1, keepdims=True))
    return soft.reshape(count, size)


def norm_parts(values):
    centred = values - jnp.mean(values, axis=1, keepdims=True)
    spread = lax.rsqrt(jnp.mean(centred * centred, axis=1, keepdims=True) + epsilon)
    return centred * spread, spread


def norm_back(gradient, normed, spread, gain):
    scaled = gradient * gain
    return spread * (
        scaled
        - jnp.mean(scaled, axis=1, keepdims=True)
        - normed * jnp.mean(scaled * normed, axis=1, keepdims=True)
    )


def run_copies(copies):
    for copy in copies:
        copy.start()
    for copy in copies:
        copy.wait()


def qkv_copies(pieces, order, kinds, target, sems, first_sem):
    rows = pieces[0].shape[1]
    copies = []
    for i, piece in enumerate(pieces):
        where = 0 if len(pieces) == 1 else pl.multiple_of(order[i] * rows, 16)
        for at, kind in enumerate(kinds):
            wide = piece.shape[2]
            copies.append(
                pltpu.make_async_copy(
                    piece.at[kind],
                    target.at[pl.ds(where, rows), pl.ds(at * wide, wide)],
                    sems.at[first_sem + len(copies)],
                )
            )
    return copies


def norm_kernel(tokens, gain, h_out, turned_out):
    normed, _ = norm_parts(tokens[...].astype(f32))
    low = (normed * gain[...]).astype(bf16)
    h_out[...] = low
    turned_out[...] = low.T


def norm_one(tokens, gain):
    rows, width = tokens.shape
    return pl.pallas_call(
        norm_kernel,
        grid=(rows // BLOCK,),
        in_specs=[by_rows(BLOCK, width), once((1, width))],
        out_specs=[by_rows(BLOCK, width), by_cols(width, BLOCK)],
        out_shape=[shaped((rows, width)), shaped((width, rows))],
        compiler_params=params(),
        cost_estimate=cost(5),
        name="norm_one",
    )(tokens, gain)


def write_state(state, state_out, pairs):
    top = first_sublanes()
    sums = []
    for p in range(pairs):
        state_out[128 * p : 128 * p + 128] = jnp.where(
            top, state[2 * p], state[2 * p + 1]
        ).astype(bf16)
        sums.append(state[2 * p, 64:65, :])
        sums.append(state[2 * p + 1, 0:1, :])
    tail = state_out.shape[0] - 128 * pairs
    sums.append(jnp.zeros((tail - 2 * pairs, 128), f32))
    state_out[128 * pairs :] = jnp.concatenate(sums, axis=0).astype(bf16)


def read_state(packed, p, h_at, pairs):
    row = 128 * pairs + 2 * p + h_at
    whole = packed[128 * p : 128 * p + 128, :]
    sums = packed[row : row + 1, :]
    sel = first_sublanes() if h_at == 0 else jnp.logical_not(first_sublanes())
    return jnp.where(sel, whole, sums)


def keys_kernel(pairs, count, more, order, h, f, signs, *refs):
    earlier, refs = refs[:more], refs[more:]
    pieces = refs[:count]
    (k_out, v_out, turned_v_out, phi_out, turned_phi_out, prefix_out, state_out) = refs[count : count + 7]
    fext, plain_out, w_kv, state, sems = refs[count + 7 :]
    step = pl.program_id(0)
    wide = 128 * pairs

    @pl.when(step == 0)
    def _():
        copies = qkv_copies(pieces, order, (1, 2), w_kv, sems, 0)
        for copy in copies:
            copy.start()
        build_maps(f, signs, fext, plain_out, pairs)
        state[...] = jnp.zeros_like(state)
        for copy in copies:
            copy.wait()

    kv_all = dot(h[...], w_kv[...]).astype(bf16)
    turned_k_all = kv_all[:, :wide].T
    turned_v_all = kv_all[:, wide:].T
    k_out[...] = turned_k_all
    v_out[...] = kv_all[:, wide:]
    turned_v_out[...] = turned_v_all
    top = first_sublanes()
    one = jnp.ones((1, 1), bf16)
    for sub in range(h.shape[0] // CHUNK):
        run = slice(CHUNK * sub, CHUNK * sub + CHUNK)
        turned_k, turned_v = turned_k_all[:, run], turned_v_all[:, run]
        prefix_out[sub] = state[...].astype(bf16)
        for p in range(pairs):
            turned_phi = soft_rows(dot(fext[p], turned_k[128 * p : 128 * p + 128])).astype(bf16)
            phi = turned_phi.T
            turned_phi_out[256 * p : 256 * p + 256, run] = turned_phi
            phi_out[run, 256 * p : 256 * p + 256] = phi
            values = turned_v[128 * p : 128 * p + 128]
            for h_at in range(2):
                sel = top if h_at == 0 else jnp.logical_not(top)
                padded = jnp.where(sel, values, one)
                state[2 * p + h_at] += dot(padded, phi[:, 128 * h_at : 128 * h_at + 128])

    @pl.when(step == pl.num_programs(0) - 1)
    def _():
        state_out[0] = earlier[0][1] if more else jnp.zeros_like(state_out[0])
        write_state(state, state_out.at[1], pairs)


def key_pass(h, weights, order, maps, signs, earlier):
    rows, width = h.shape
    pairs = maps.shape[1] // 2
    wide = 128 * pairs
    count = rows // CHUNK
    packed = wide + 16
    return list(
        pl.pallas_call(
            functools.partial(keys_kernel, pairs, len(weights), len(earlier)),
            grid=(rows // BLOCK,),
            in_specs=[
                scalars,
                by_rows(BLOCK, width),
                map_block(maps, 1),
                once(signs.shape),
            ]
            + [once((2, packed, 128))] * len(earlier)
            + [anywhere] * len(weights),
            out_specs=[
                by_cols(wide, BLOCK),
                by_rows(BLOCK, wide),
                by_cols(wide, BLOCK),
                by_rows(BLOCK, 2 * wide),
                by_cols(2 * wide, BLOCK),
                pl.BlockSpec((BLOCK // CHUNK, 2 * pairs, 128, 128), lambda c: (c, 0, 0, 0)),
                once((2, packed, 128)),
                once((pairs, 256, 128)),
                once((pairs, 128, 256)),
            ],
            out_shape=[
                shaped((wide, rows)),
                shaped((rows, wide)),
                shaped((wide, rows)),
                shaped((rows, 2 * wide)),
                shaped((2 * wide, rows)),
                shaped((count, 2 * pairs, 128, 128)),
                shaped((2, packed, 128)),
                shaped((pairs, 256, 128)),
                shaped((pairs, 128, 256)),
            ],
            scratch_shapes=[
                pltpu.VMEM((width, 2 * wide), bf16),
                pltpu.VMEM((2 * pairs, 128, 128), f32),
                pltpu.SemaphoreType.DMA((2 * len(weights),)),
            ],
            compiler_params=params(),
            cost_estimate=cost(10),
            name="key_pass",
        )(order, h, maps, signs, *earlier, *weights)
    )


def query_kernel(pairs, count, order, h, turned_k_phi, v, prefix, f, signs, *refs):
    pieces = refs[:count]
    q_out, phi_out, turned_phi_out, numer_out, fext, plain_out, w_q, sems = refs[count:]

    @pl.when(pl.program_id(0) == 0)
    def _():
        copies = qkv_copies(pieces, order, (0,), w_q, sems, 0)
        for copy in copies:
            copy.start()
        build_maps(f, signs, fext, plain_out, pairs)
        for copy in copies:
            copy.wait()

    turned_q_all = dot(h[...], w_q[...]).astype(bf16).T
    q_out[...] = turned_q_all
    first = first_lanes()
    one = jnp.ones((1, 1), bf16)
    size = CHUNK
    past = lax.broadcasted_iota(jnp.int32, (size, size), 0) >= lax.broadcasted_iota(
        jnp.int32, (size, size), 1
    )
    for sub in range(h.shape[0] // CHUNK):
        run = slice(CHUNK * sub, CHUNK * sub + CHUNK)
        turned_q = turned_q_all[:, run]
        for p in range(pairs):
            turned_phi = soft_rows(dot(fext[p], turned_q[128 * p : 128 * p + 128])).astype(bf16)
            phi = turned_phi.T
            turned_phi_out[256 * p : 256 * p + 256, run] = turned_phi
            phi_out[run, 256 * p : 256 * p + 256] = phi
            v_two = v[run, 128 * p : 128 * p + 128]
            for h_at in range(2):
                at = 256 * p + 128 * h_at
                sel = first if h_at == 0 else jnp.logical_not(first)
                padded = jnp.where(sel, v_two, one)
                phi_q = phi[:, 128 * h_at : 128 * h_at + 128]
                scores = dot(phi_q, turned_k_phi[at : at + 128, run])
                scores = jnp.where(past, scores, 0.0).astype(bf16)
                numer_out[run, at : at + 128] = (
                    dot(scores, padded) + dot_t(phi_q, prefix[sub, 2 * p + h_at])
                ).astype(bf16)


def query_pass(h, weights, order, turned_k_phi, v, prefix, maps, signs):
    rows, width = h.shape
    pairs = maps.shape[1] // 2
    wide = 128 * pairs
    return list(
        pl.pallas_call(
            functools.partial(query_kernel, pairs, len(weights)),
            grid=(rows // BLOCK,),
            in_specs=[
                scalars,
                by_rows(BLOCK, width),
                by_cols(2 * wide, BLOCK),
                by_rows(BLOCK, wide),
                pl.BlockSpec((BLOCK // CHUNK, 2 * pairs, 128, 128), lambda c: (c, 0, 0, 0)),
                map_block(maps, 0),
                once(signs.shape),
            ]
            + [anywhere] * len(weights),
            out_specs=[
                by_cols(wide, BLOCK),
                by_rows(BLOCK, 2 * wide),
                by_cols(2 * wide, BLOCK),
                by_rows(BLOCK, 2 * wide),
                once((pairs, 256, 128)),
                once((pairs, 128, 256)),
            ],
            out_shape=[
                shaped((wide, rows)),
                shaped((rows, 2 * wide)),
                shaped((2 * wide, rows)),
                shaped((rows, 2 * wide)),
                shaped((pairs, 256, 128)),
                shaped((pairs, 128, 256)),
            ],
            scratch_shapes=[
                pltpu.VMEM((width, wide), bf16),
                pltpu.SemaphoreType.DMA((len(weights),)),
            ],
            compiler_params=params(),
            cost_estimate=cost(15),
            name="query_pass",
        )(order, h, turned_k_phi, v, prefix, maps, signs, *weights)
    )


def quarter_copies(pieces, order, target, first_row, rows, sems, first_sem):
    copies = []
    for i, piece in enumerate(pieces):
        where = pl.multiple_of(order[6 + i] * rows, 16)
        copies.append(
            pltpu.make_async_copy(
                piece.at[pl.ds(first_row, rows)],
                target.at[pl.ds(where, rows)],
                sems.at[first_sem + i],
            )
        )
    return copies


def front_kernel(pairs, units, order, tokens, *refs):
    numer, phi = refs[:2], refs[2:4]
    incoming, gain, wo_any = refs[4:7]
    pieces = refs[7:11]
    attended_out, turned_a_out, inverse_out, resid_out, h_out, turned_h_out = refs[11:17]
    held, wo_own, wo_oth, sems = refs[17:]
    first = first_lanes()
    wide = 128 * pairs
    start = pl.program_id(0) == 0

    def weight_copies():
        return [pltpu.make_async_copy(wo_any, wo_own, sems.at[0])] + quarter_copies(
            pieces, order, wo_oth, units // 4, wide // 4, sems, 1
        )

    @pl.when(start)
    def _():
        for copy in weight_copies():
            copy.start()
        for half in range(2):
            for p in range(pairs):
                for h_at in range(2):
                    held[half, 2 * p + h_at] = read_state(
                        incoming.at[half], p, h_at, pairs
                    ).astype(bf16)

    for half in range(2):
        for p in range(pairs):
            sums = []
            for h_at in range(2):
                at = 256 * p + 128 * h_at
                sums.append(
                    numer[half][:, at : at + 128].astype(f32)
                    + dot_t(phi[half][:, at : at + 128], held[half, 2 * p + h_at])
                )
            numerator = jnp.where(first, sums[0], sums[1])
            swapped = 1.0 / jnp.where(first, sums[1], sums[0])
            inv = pltpu.roll(swapped, 64, 1)
            attended = (numerator * inv).astype(bf16)
            at = wide * half + 128 * p
            inverse_out[:, at : at + 128] = inv.astype(bf16)
            attended_out[:, at : at + 128] = attended
            turned_a_out[at : at + 128, :] = attended.T

    @pl.when(start)
    def _():
        for copy in weight_copies():
            copy.wait()

    resid = (
        tokens[...].astype(f32)
        + dot(attended_out[:, :wide], wo_own[...])
        + dot(attended_out[:, wide:], wo_oth[...])
    )
    resid_out[...] = resid.astype(bf16)
    normed, _ = norm_parts(resid)
    h_two = (normed * gain[...]).astype(bf16)
    h_out[...] = h_two
    turned_h_out[...] = h_two.T


def front_pass(order, tokens, numers, phis, incoming, gain, w_out, pieces, block):
    rows, width = tokens.shape
    wide = w_out.shape[0]
    pairs = wide // 128
    units = 4 * pieces[0].shape[0] - wide
    return pl.pallas_call(
        functools.partial(front_kernel, pairs, units),
        grid=(rows // block,),
        in_specs=[scalars, by_rows(block, width)]
        + [by_rows(block, 2 * wide)] * 4
        + [once(incoming.shape), once(gain.shape)]
        + [anywhere] * 5,
        out_specs=[
            by_rows(block, 2 * wide),
            by_cols(2 * wide, block),
            by_rows(block, 2 * wide),
            by_rows(block, width),
            by_rows(block, width),
            by_cols(width, block),
        ],
        out_shape=[
            shaped((rows, 2 * wide)),
            shaped((2 * wide, rows)),
            shaped((rows, 2 * wide)),
            shaped((rows, width)),
            shaped((rows, width)),
            shaped((width, rows)),
        ],
        scratch_shapes=[
            pltpu.VMEM((2, 2 * pairs, 128, 128), bf16),
            pltpu.VMEM((wide, width), bf16),
            pltpu.VMEM((wide, width), bf16),
            pltpu.SemaphoreType.DMA((5,)),
        ],
        compiler_params=params(),
        cost_estimate=cost(13),
        name="front_pass",
    )(order, tokens, *numers, *phis, incoming, gain, w_out, *pieces)


def feed_forward(pre):
    square = pre * pre
    swing = jnp.tanh(GELU_A * pre * (1.0 + GELU_B * square))
    half_up = 0.5 + 0.5 * swing
    slope = half_up + (0.5 * GELU_A) * pre * (1.0 - swing * swing) * (
        1.0 + (3.0 * GELU_B) * square
    )
    return (pre * half_up).astype(bf16), slope


def add_to(total, part):
    return part if total is None else total + part


def feed_kernel(tile, order, h_any, turned_any, d_any, *refs):
    ups, downs = refs[:4], refs[4:8]
    sums_out = (refs[8:10], refs[10:12])
    mixed_out, grad_out = refs[12:14]
    h, turned, d, up, down, mixed, grad_h, act, grad_pre, mixed_low, grad_low = refs[14:25]
    sums, sems, out_sems = refs[25:]
    step = pl.program_id(0)
    rows = h.shape[0]
    part = up.shape[2]
    quarter = part // 2
    block = 512
    blocks = rows // block

    def chunk_copies(at):
        run = pl.ds(block * at, block)
        return [
            pltpu.make_async_copy(h_any.at[run], h.at[run], sems.at[8 + 2 * at]),
            pltpu.make_async_copy(d_any.at[run], d.at[run], sems.at[9 + 2 * at]),
        ]

    def weight_copies(spot):
        copies = []
        for i in (2, 3) if spot == 0 else (0, 1):
            where = pl.multiple_of(order[2 + i] % 2 * quarter, 128)
            copies.append(
                pltpu.make_async_copy(
                    ups[i], up.at[spot, :, pl.ds(where, quarter)], sems.at[2 * i]
                )
            )
            where = pl.multiple_of(order[6 + i] % 2 * quarter, 16)
            copies.append(
                pltpu.make_async_copy(
                    downs[i].at[pl.ds(0, quarter)],
                    down.at[spot, pl.ds(where, quarter)],
                    sems.at[2 * i + 1],
                )
            )
        return copies

    def turned_copy():
        return pltpu.make_async_copy(turned_any, turned, sems.at[8 + 2 * blocks])

    def part_copies(at):
        run = pl.ds(block * at, block)
        return [
            pltpu.make_async_copy(mixed_low.at[run], mixed_out.at[run], out_sems.at[2 * at]),
            pltpu.make_async_copy(grad_low.at[run], grad_out.at[run], out_sems.at[2 * at + 1]),
        ]

    def sum_copies(spot):
        return [
            pltpu.make_async_copy(
                sums.at[spot, i], sums_out[spot][i], out_sems.at[2 * blocks + 2 * spot + i]
            )
            for i in range(2)
        ]

    @pl.when(step == 0)
    def _():
        for copy in weight_copies(0) + chunk_copies(0):
            copy.start()
        for at in range(1, blocks):
            for copy in chunk_copies(at):
                copy.start()
        turned_copy().start()
        for copy in weight_copies(1):
            copy.start()
        for copy in weight_copies(0):
            copy.wait()

    @pl.when(step == 1)
    def _():
        for copy in weight_copies(1):
            copy.wait()

    for at in range(blocks):
        run = slice(block * at, block * at + block)

        @pl.when(step == 0)
        def _(at=at):
            for copy in chunk_copies(at):
                copy.wait()

        mixed_part = grad_part = None
        for sub in range(0, part, tile):
            up_tile = up[step, :, sub : sub + tile]
            down_tile = down[step, sub : sub + tile, :]
            low, slope = feed_forward(dot(h[run, :], up_tile))
            grad = (dot_t(d[run, :], down_tile) * slope).astype(bf16)
            act[sub : sub + tile, run] = low.T
            grad_pre[run, sub : sub + tile] = grad
            mixed_part = add_to(mixed_part, dot(low, down_tile))
            grad_part = add_to(grad_part, dot_t(grad, up_tile))

        @pl.when(step == 0)
        def _(run=run, mixed_part=mixed_part, grad_part=grad_part):
            mixed[run, :] = mixed_part
            grad_h[run, :] = grad_part

        @pl.when(step == 1)
        def _(at=at, run=run, mixed_part=mixed_part, grad_part=grad_part):
            mixed_low[run, :] = (mixed[run, :] + mixed_part).astype(bf16)
            grad_low[run, :] = (grad_h[run, :] + grad_part).astype(bf16)
            for copy in part_copies(at):
                copy.start()

    @pl.when(step == 0)
    def _():
        turned_copy().wait()

    sums[step, 1] = dot(act[...], d[...]).astype(bf16)
    sums[step, 0] = dot(turned[...], grad_pre[...]).astype(bf16)

    @pl.when(step == 0)
    def _():
        for copy in sum_copies(0):
            copy.start()

    @pl.when(step == 1)
    def _():
        for copy in sum_copies(1):
            copy.start()
        for at in range(blocks):
            for copy in part_copies(at):
                copy.wait()
        for copy in sum_copies(0) + sum_copies(1):
            copy.wait()


def feed_pass(order, h, turned_h, d_out, ups, downs, tile):
    rows, width = h.shape
    part = 2 * ups[0].shape[1]
    square = (width, part)
    blocks = rows // 512
    return pl.pallas_call(
        functools.partial(feed_kernel, tile),
        grid=(2,),
        in_specs=[scalars] + [anywhere] * 11,
        out_specs=[anywhere] * 6,
        out_shape=[shaped(square), shaped((part, width))] * 2 + [shaped((rows, width))] * 2,
        scratch_shapes=[
            pltpu.VMEM((rows, width), bf16),
            pltpu.VMEM((width, rows), bf16),
            pltpu.VMEM((rows, width), bf16),
            pltpu.VMEM((2, width, part), bf16),
            pltpu.VMEM((2, part, width), bf16),
            pltpu.VMEM((rows, width), f32),
            pltpu.VMEM((rows, width), f32),
            pltpu.VMEM((part, rows), bf16),
            pltpu.VMEM((rows, part), bf16),
            pltpu.VMEM((rows, width), bf16),
            pltpu.VMEM((rows, width), bf16),
            pltpu.VMEM((2, 2, width, part), bf16),
            pltpu.SemaphoreType.DMA((9 + 2 * blocks,)),
            pltpu.SemaphoreType.DMA((4 + 2 * blocks,)),
        ],
        compiler_params=params(),
        cost_estimate=cost(32),
        name="feed_pass",
    )(order, h, turned_h, d_out, *ups, *downs)


def middle_kernel(pairs, tile, order, resid, h, d_out, *refs):
    mixed_part, grad_part, attended, inverse = refs[:4]
    phi = refs[4:6]
    gain, cross, wo_any, up_any, down_any = refs[6:11]
    pieces = refs[11:15]
    (
        act_out,
        pre_out,
        mixed_out,
        resid_out,
        gn_out,
        gd_out,
        turned_n_out,
        turned_d_out,
        state_out,
    ) = refs[15:24]
    state, wo_own, up, down, wo_oth, sems = refs[24:]
    step = pl.program_id(0)
    top = first_sublanes()
    wide = 128 * pairs
    units = up.shape[1]

    def early_copies():
        return [
            pltpu.make_async_copy(up_any, up, sems.at[0]),
            pltpu.make_async_copy(down_any, down, sems.at[1]),
        ]

    def late_copies():
        return [pltpu.make_async_copy(wo_any, wo_own, sems.at[2])] + quarter_copies(
            pieces, order, wo_oth, units // 4, wide // 4, sems, 3
        )

    @pl.when(step == 0)
    def _():
        for copy in early_copies() + late_copies():
            copy.start()
        state[...] = jnp.zeros_like(state)
        for copy in early_copies():
            copy.wait()

    h_two = h[...]
    d_low = d_out[...]
    mixed = grad_h = None
    for at in range(0, units, tile):
        low, slope = feed_forward(dot(h_two, up[:, at : at + tile]))
        grad_pre = (dot_t(d_low, down[at : at + tile, :]) * slope).astype(bf16)
        act_out[at : at + tile, :] = low.T
        for col in range(at, at + tile, 256):
            pre_out[col // 768, :, col % 768 : col % 768 + 256] = grad_pre[
                :, col - at : col - at + 256
            ]
        mixed = add_to(mixed, dot(low, down[at : at + tile, :]))
        grad_h = add_to(grad_h, dot_t(grad_pre, up[:, at : at + tile]))
    summed = resid[...].astype(f32)
    normed, spread = norm_parts(summed)
    mixed_out[...] = (summed + mixed_part[...].astype(f32) + mixed).astype(bf16)
    grad_h = grad_part[...].astype(f32) + grad_h
    grad_resid = (d_low.astype(f32) + norm_back(grad_h, normed, spread, gain[...])).astype(bf16)
    resid_out[...] = grad_resid

    @pl.when(step == 0)
    def _():
        for copy in late_copies():
            copy.wait()

    for half in range(2):
        grad_att = dot_t(grad_resid, (wo_own, wo_oth)[half][...]).astype(bf16).astype(f32)
        for p in range(pairs):
            at = wide * half + 128 * p
            own = grad_att[:, 128 * p : 128 * p + 128]
            scaled = own * inverse[:, at : at + 128].astype(f32)
            grad_n = scaled.astype(bf16)
            exact = attended[:, at : at + 128].astype(f32)
            grad_d = dot((scaled * exact).astype(bf16), cross[...]).astype(bf16)
            gn_out[:, at : at + 128] = grad_n
            gd_out[:, at : at + 128] = grad_d
            turned_n = grad_n.T
            turned_d = grad_d.T
            turned_n_out[at : at + 128, :] = turned_n
            turned_d_out[at : at + 128, :] = turned_d
            left = jnp.concatenate([turned_n, turned_d[0:16], turned_d[64:80]], axis=0)
            sums = dot(left, phi[half][:, 256 * p : 256 * p + 256])
            state[half, 128 * p : 128 * p + 128] += jnp.where(
                top, sums[:128, :128], sums[:128, 128:]
            )
            row = wide + 2 * p
            state[half, row : row + 1] += sums[144:145, :128]
            state[half, row + 1 : row + 2] += sums[128:129, 128:]

    @pl.when(step == pl.num_programs(0) - 1)
    def _():
        state_out[...] = state[...].astype(bf16)


def middle_pass(
    order, resid, h_two, d_out, parts, attended, inverse, phis, gain, cross, owns, pieces, packed, block, tile
):
    rows, width = resid.shape
    wide = owns[0].shape[0]
    pairs = wide // 128
    units = owns[1].shape[1]
    cols_out = [width, width, 2 * wide, 2 * wide]
    spots = units // 768
    return pl.pallas_call(
        functools.partial(middle_kernel, pairs, tile),
        grid=(rows // block,),
        in_specs=[scalars]
        + [by_rows(block, width)] * 5
        + [by_rows(block, 2 * wide)] * 4
        + [once(gain.shape), once(cross.shape)]
        + [anywhere] * 7,
        out_specs=[by_cols(units, block), pl.BlockSpec((spots, block, 768), lambda c: (0, c, 0))]
        + [by_rows(block, c) for c in cols_out]
        + [by_cols(2 * wide, block)] * 2
        + [once(packed)],
        out_shape=[shaped((units, rows)), shaped((spots, rows, 768))]
        + [shaped((rows, c)) for c in cols_out]
        + [shaped((2 * wide, rows))] * 2
        + [shaped(packed)],
        scratch_shapes=[
            pltpu.VMEM(packed, f32),
            pltpu.VMEM((wide, width), bf16),
            pltpu.VMEM((width, units), bf16),
            pltpu.VMEM((units, width), bf16),
            pltpu.VMEM((wide, width), bf16),
            pltpu.SemaphoreType.DMA((7,)),
        ],
        compiler_params=params(),
        cost_estimate=cost(35),
        name="middle_pass",
    )(order, resid, h_two, d_out, *parts, attended, inverse, *phis, gain, cross, *owns, *pieces)


def up_kernel(core, left, right, got, out):
    product = dot(left[...], right[0])
    mine = pl.program_id(0) == core[0]

    @pl.when(mine)
    def _():
        out[...] = (product + got[...].astype(f32)).astype(bf16)

    @pl.when(jnp.logical_not(mine))
    def _():
        out[...] = product.astype(bf16)


def up_pass(core, left, right, got):
    width, rows = left.shape
    count, _, part = right.shape
    return pl.pallas_call(
        up_kernel,
        grid_spec=pltpu.PrefetchScalarGridSpec(
            num_scalar_prefetch=1,
            grid=(count,),
            in_specs=[
                once((width, rows)),
                pl.BlockSpec((1, rows, part), lambda s, c: (s, 0, 0)),
                once((width, part)),
            ],
            out_specs=pl.BlockSpec((width, part), lambda s, c: (0, s)),
        ),
        out_shape=shaped((width, count * part)),
        compiler_params=params(),
        cost_estimate=cost(8),
        name="up_pass",
    )(core, left, right, got)


def down_kernel(core, left, right, own_left, oth_left, right_more, out, more_out):
    out[...] = dot(left[...], right[...]).astype(bf16)
    for side, rows in enumerate((own_left, oth_left)):
        more_out[side] = dot(rows[...], right_more[...]).astype(bf16)


def down_pass(half, left, right, left_more, right_more):
    rows, width = right.shape
    part = left.shape[0] // 2
    more = left_more.shape[0] // 4
    tile = width // 2
    cols = pl.BlockSpec((rows, tile), lambda s, half: (0, s))
    mine = lambda count, first: pl.BlockSpec((count, rows), lambda s, half: (first + half[0], 0))
    return pl.pallas_call(
        down_kernel,
        grid_spec=pltpu.PrefetchScalarGridSpec(
            num_scalar_prefetch=1,
            grid=(2,),
            in_specs=[mine(part, 0), cols, mine(more, 0), mine(more, 2), cols],
            out_specs=[
                pl.BlockSpec((part, tile), lambda s, half: (0, s)),
                pl.BlockSpec((2, more, tile), lambda s, half: (0, s, 0)),
            ],
        ),
        out_shape=[shaped((part, width)), shaped((2, 2 * more, tile))],
        compiler_params=params(),
        cost_estimate=cost(8),
        name="down_pass",
    )(half, left, right, left_more, left_more, right_more)


def back_kernel(pairs, at_pair, more, core, *refs):
    sides = (refs[:15], refs[15:30])
    incoming, later, ones, h_any = refs[30:34]
    earlier = refs[34 : 34 + more]
    grad_outs = refs[34 + more : 36 + more]
    send_out, keep_out, map_out = refs[36 + more : 39 + more]
    held, state, grads, maps, turned_h, sem = refs[39 + more :]
    step = pl.program_id(0)
    last = pl.num_programs(0) - 1
    first = first_lanes()
    top = first_sublanes()
    size = CHUNK
    inner = refs[2].shape[0] // CHUNK
    past = lax.broadcasted_iota(jnp.int32, (size, size), 0) >= lax.broadcasted_iota(
        jnp.int32, (size, size), 1
    )
    one = jnp.ones((1, 1), bf16)

    @pl.when(step == 0)
    def _():
        pltpu.make_async_copy(h_any, turned_h, sem.at[0]).start()
        maps[...] = jnp.zeros_like(maps)
        for side in range(2):
            for h_at in range(2):
                held[side, h_at] = read_state(incoming.at[side], at_pair, h_at, pairs)
                state[side, h_at] = read_state(later.at[side], at_pair, h_at, pairs)

    for sub in reversed(range(inner)):
        run = slice(CHUNK * sub, CHUNK * sub + CHUNK)
        for side in range(2):
            (q, k, v, turned_v, pq, turned_pq, pk, turned_pk) = sides[side][:8]
            (gn, gd, turned_n, turned_d, prefix, fq, fk) = sides[side][8:]
            grads_q, grads_k, grads_v = [], [], []
            for h_at in range(2):
                sel = first if h_at == 0 else jnp.logical_not(first)
                sel_top = top if h_at == 0 else jnp.logical_not(top)
                lanes = slice(128 * h_at, 128 * h_at + 128)
                padded_v = jnp.where(sel, v[run, :], one)
                padded_vt = jnp.where(sel_top, turned_v[:, run], one)
                padded_g = jnp.where(sel, gn[run, :], gd[run, :])
                padded_gt = jnp.where(sel_top, turned_n[:, run], turned_d[:, run])
                before = (prefix[sub, h_at].astype(f32) + held[side, h_at]).astype(bf16)
                after = state[side, h_at].astype(bf16)
                e = jnp.where(past, dot_t(padded_g, padded_v), 0.0).astype(bf16)
                s = jnp.where(past, dot(pq[run, lanes], turned_pk[lanes, run]), 0.0).astype(bf16)
                grads_q.append(dot(e, pk[run, lanes]) + dot(padded_g, before))
                grads_k.append(dot(turned_pq[lanes, run], e) + dot(after.T, padded_vt))
                grads_v.append(dot(padded_gt, s) + dot(after, turned_pk[lanes, run]))
                state[side, h_at] += dot(padded_gt, pq[run, lanes])

            grad_phi = jnp.concatenate(grads_q, axis=1)
            phi = pq[run, :].astype(f32)
            shared = dot((phi * grad_phi).astype(bf16), ones[...])
            grad_u = (phi * (grad_phi - shared)).astype(bf16)
            maps[side, 0] += dot(q[:, run], grad_u)
            grad_q = dot_t(grad_u, fq[0]).astype(bf16)

            grad_phi = jnp.concatenate(grads_k, axis=0).reshape(4, 64, size)
            phi = turned_pk[:, run].astype(f32).reshape(4, 64, size)
            shared = jnp.sum(phi * grad_phi, axis=1, keepdims=True)
            grad_u = (phi * (grad_phi - shared)).reshape(256, size).astype(bf16)
            maps[side, 1] += dot_t(k[:, run], grad_u)
            grad_k = dot(fk[0], grad_u).astype(bf16).T
            grad_v = jnp.where(top, grads_v[0], grads_v[1]).astype(bf16).T

            joined = jnp.concatenate([grad_q, grad_k, grad_v], axis=1)
            grad_outs[side][run, :] = joined
            where = pl.multiple_of(((last - step) * inner + sub) * size, size)
            grads[pl.ds(where, size), 384 * side : 384 * side + 384] = joined

    @pl.when(step == last)
    def _():
        pltpu.make_async_copy(h_any, turned_h, sem.at[0]).wait()
        product = dot(turned_h[...], grads[...]).astype(bf16)
        part = product.shape[0] // 2
        mine = core[0] == 0
        for side in range(2):
            cols = slice(384 * side, 384 * side + 384)
            low, high = product[:part, cols], product[part:, cols]
            send_out[side, 0:part] = jnp.where(mine, high, low)
            keep_out[side, 0:part] = jnp.where(mine, low, high)
            joins = [
                jnp.where(top, maps[side, i][:, :128], maps[side, i][:, 128:]) for i in range(2)
            ]
            turns = [pltpu.roll(j, 64, 1) for j in joins]
            own_map = jnp.where(first, joins[0] - turns[0], turns[1] - joins[1]).astype(bf16)
            map_out[side] = own_map
            if more:
                whole = jnp.concatenate([m[side] for m in earlier] + [own_map], axis=1)
                low, high = whole[:64], whole[64:]
                send_out[side, part : part + 64] = jnp.where(mine, high, low)
                keep_out[side, part : part + 64] = jnp.where(mine, low, high)
                send_out[side, part + 64 :] = jnp.zeros_like(low)
                keep_out[side, part + 64 :] = jnp.zeros_like(low)


def back_pass(at, core, sides, seconds, prefix, incoming, later, fq, fk, ones, turned_h, earlier):
    rows = sides[0][2].shape[0]
    pairs = fq[0].shape[0]
    width = turned_h.shape[0]
    count = rows // BLOCK
    here = lambda cols, spot: pl.BlockSpec((BLOCK, cols), lambda c, core: (count - 1 - c, spot))
    turned = lambda cols, spot: pl.BlockSpec((cols, BLOCK), lambda c, core: (spot, count - 1 - c))
    weights = pl.BlockSpec((1, 128, 256), lambda c, core: (at, 0, 0))
    states = pl.BlockSpec(
        (BLOCK // CHUNK, 2, 128, 128), lambda c, core: (count - 1 - c, at, 0, 0)
    )
    more = len(earlier)
    sums = (2, width // 2 + (128 if more else 0), 384)
    in_specs, args = [], []
    for side in range(2):
        both = pairs * side + at
        in_specs += [turned(128, at), turned(128, at), here(128, at), turned(128, at)]
        in_specs += [here(256, at), turned(256, at)] * 2
        in_specs += [here(128, both)] * 2 + [turned(128, both)] * 2
        in_specs += [states, weights, weights]
        args += [*sides[side], *seconds, prefix[side], fq[side], fk[side]]
    return pl.pallas_call(
        functools.partial(back_kernel, pairs, at, more),
        grid_spec=pltpu.PrefetchScalarGridSpec(
            num_scalar_prefetch=1,
            grid=(count,),
            in_specs=in_specs
            + [once(incoming.shape)] * 2
            + [once(ones.shape), anywhere]
            + [once((2, 128, 128))] * more,
            out_specs=[here(384, 0)] * 2 + [once(sums)] * 2 + [once((2, 128, 128))],
            scratch_shapes=[
                pltpu.VMEM((2, 2, 128, 128), f32),
                pltpu.VMEM((2, 2, 128, 128), f32),
                pltpu.VMEM((rows, 768), bf16),
                pltpu.VMEM((2, 2, 128, 256), f32),
                pltpu.VMEM((width, rows), bf16),
                pltpu.SemaphoreType.DMA((1,)),
            ],
        ),
        out_shape=[shaped((rows, 384))] * 2 + [shaped(sums)] * 2 + [shaped((2, 128, 128))],
        compiler_params=params(),
        cost_estimate=cost(17),
        name="back_pass",
    )(core, *args, incoming, later, ones, turned_h, *earlier)


def tokens_kernel(pairs, count, order, tokens, resid, gain, *refs):
    pieces = refs[: 1 + count]
    grads = refs[1 + count : 1 + count + 2 * pairs]
    out, w_own, w_oth, sems = refs[1 + count + 2 * pairs :]

    @pl.when(pl.program_id(0) == 0)
    def _():
        copies = qkv_copies(pieces[:1], order, (0, 1, 2), w_own, sems, 0)
        copies += qkv_copies(pieces[1:], order, (0, 1, 2), w_oth, sems, 3)
        run_copies(copies)

    normed, spread = norm_parts(tokens[...].astype(f32))
    total = None
    for half in range(2):
        joined = jnp.concatenate(
            [
                g[:, 128 * kind : 128 * kind + 128]
                for kind in range(3)
                for g in grads[half * pairs : half * pairs + pairs]
            ],
            axis=1,
        )
        part = dot_t(joined, (w_own, w_oth)[half][...])
        total = part if total is None else total + part
    back = norm_back(total, normed, spread, gain[...])
    out[...] = (resid[...].astype(f32) + back).astype(bf16)


def tokens_pass(order, tokens, resid, gain, w_own, pieces, grads, block, first, blocks, done=None):
    rows, width = tokens.shape
    pairs = len(grads) // 2
    cols = 3 * w_own.shape[2]
    count = len(pieces)
    cut = lambda cols: pl.BlockSpec((block, cols), lambda c: (first + c, 0))
    operands = [order, tokens, resid, gain, w_own, *pieces, *grads]
    more = [] if done is None else [done]

    def kernel(*refs):
        refs = list(refs)
        if more:
            del refs[len(operands)]
        tokens_kernel(pairs, count, *refs)

    return pl.pallas_call(
        kernel,
        grid=(blocks,),
        in_specs=[scalars]
        + [cut(width)] * 2
        + [once(gain.shape)]
        + [anywhere] * (1 + count)
        + [cut(384)] * len(grads)
        + [anywhere] * len(more),
        out_specs=cut(width),
        out_shape=shaped((rows, width)),
        input_output_aliases={len(operands): 0} if more else {},
        scratch_shapes=[
            pltpu.VMEM((width, cols), bf16),
            pltpu.VMEM((width, cols), bf16),
            pltpu.SemaphoreType.DMA((3 + 3 * count,)),
        ],
        compiler_params=params(),
        cost_estimate=cost(8),
        name="tokens_pass",
    )(*operands, *more)


def cross_to(value, axis, flip):
    count = lax.axis_size(axis)
    return lax.ppermute(value, axis, [(i, i ^ flip) for i in range(count)])


def swap(value, axis, bit):
    return cross_to(value, axis, 1 << bit)


def bit_of(axis, bit):
    return (lax.axis_index(axis) >> bit) & 1


def bits_of(axis):
    return lax.axis_size(axis).bit_length() - 1


def ordered(bit, mine, theirs, axis=0):
    return jnp.where(
        bit == 0,
        jnp.concatenate([mine, theirs], axis),
        jnp.concatenate([theirs, mine], axis),
    )


def add_low(*parts):
    total = parts[0].astype(f32)
    for part in parts[1:]:
        total = total + part.astype(f32)
    return total.astype(bf16)


class Flow:
    def __init__(self):
        self.ready = {}
        self.steps = {}
        self.done = {}

    def start(self, name, steps):
        self.steps[name] = steps
        self.ready[name] = next(steps)

    def slot(self, names, others):
        names = [n for n in names if n in self.steps]
        tied, others = lax.optimization_barrier(([self.ready[n] for n in names], others))
        for name, value in zip(names, tied):
            self.move(name, value)
        return others

    def move(self, name, value):
        try:
            self.ready[name] = self.steps[name].send(value)
        except StopIteration as end:
            self.done[name] = end.value
            del self.steps[name], self.ready[name]

    def finish(self, names):
        for name in names:
            while name in self.steps:
                self.move(name, self.ready[name])


def fetch_halves(weight, axis):
    count = weight.shape[axis] // 2
    part = yield lax.dynamic_slice_in_dim(weight, bit_of("ctx", 0) * count, count, axis)
    part = yield swap(part, "heads", 0)
    return [part, swap(part, "ctx", 0)]


def fetch_quarters(weights, across, axis):
    place = 2 * bit_of("ctx", 0) + bit_of(*across)
    parts = []
    for weight in weights:
        count = weight.shape[axis] // 4
        parts.append(lax.dynamic_slice_in_dim(weight, place * count, count, axis))
    part = yield jnp.concatenate(parts, axis)
    part = yield swap(part, "heads", 0)
    part, second, third = yield part, swap(part, *across), swap(part, "ctx", 0)
    return [part, second, third, swap(second, "ctx", 0)]


def fetch_order():
    core = bit_of("ctx", 0)
    order = [core, 1 - core]
    for across in (bit_of("ctx", 1), bit_of("batch", 0)):
        order += [
            2 * core + across,
            2 * core + 1 - across,
            2 - 2 * core + across,
            3 - 2 * core - across,
        ]
    return jnp.stack(order).astype(jnp.int32)


def reduce_sums(send, keep, ways, spread=False):
    send = yield send
    got = swap(send, "ctx", 0)
    left, oth = add_low(keep[0], got[0]), add_low(keep[1], got[1])
    return (yield from reduce_tail(left, [swap(oth, "heads", 0)], ways, spread))


def send_over(send, keep):
    send = yield send
    total = yield add_low(keep, swap(send, "ctx", 0))
    return (yield swap(total, "heads", 0))


def send_over_late(send, keep):
    send = yield send
    got = swap(send, "ctx", 0)
    count = keep.shape[0] // 2
    first, rest = yield [add_low(keep[i], got[i]) for i in (slice(0, count), slice(count, None))]
    first, rest = yield swap(first, "heads", 0), rest
    rest = yield rest
    return jnp.concatenate([first, (yield swap(rest, "heads", 0))])


def reduce_tail(left, rights, ways, spread=False):
    stages = [("ctx", b, 1) for b in range(1, bits_of("ctx"))]
    count = bits_of("batch")
    along = [("batch", b, min(ways, count - b)) for b in range(0, count, ways)]
    if not spread:
        stages += along
    for axis, low_bit, bits in stages:
        ways = 1 << bits
        place = (lax.axis_index(axis) >> low_bit) & (ways - 1)
        count = left.shape[0] // ways
        cut = lambda at: add_low(
            *[lax.dynamic_slice_in_dim(a, at * count, count, 0) for a in (left, *rights)]
        )
        sends = [cut(place ^ flip) for flip in range(1, ways)]
        left, sends = yield (cut(place), sends)
        rights = [cross_to(s, axis, (i + 1) << low_bit) for i, s in enumerate(sends)]
    whole = add_low(left, *rights)
    for axis, low_bit, bits in along if spread else []:
        whole = yield whole
        got = [cross_to(whole, axis, flip << low_bit) for flip in range(1, 1 << bits)]
        whole = add_low(whole, *got)
    for axis, low_bit, bits in reversed(stages):
        whole = yield whole
        parts = [whole] + [cross_to(whole, axis, flip << low_bit) for flip in range(1, 1 << bits)]
        for b in range(bits):
            bit = bit_of(axis, low_bit + b)
            parts = [ordered(bit, parts[i], parts[i + 1]) for i in range(0, len(parts), 2)]
        whole = parts[0]
    whole = yield whole
    return (yield (whole, swap(whole, "ctx", 0)))


def send_once(value, axis, bit):
    value = yield value
    return swap(value, axis, bit)


def scan_runs(total, boundary, rows, backward):
    place, side = lax.axis_index("ctx"), lax.axis_index("heads")
    second = lambda spot, half: (2 * spot + half) * rows >= boundary
    end = 0 if backward else 1
    total = yield total
    got = jnp.flip(swap(total, "heads", 0).astype(f32), 0)
    total = total.astype(f32)
    mine = second(place, side)
    joins = second(place, 0) == second(place, 1)
    received = jnp.where(jnp.logical_and(side == end, joins), got, 0.0)
    near = jnp.where(side == end, total, got)
    far = jnp.where(side == end, got, total)
    low = yield (near + jnp.where(joins, far, 0.0)).astype(bf16)
    for flip in range(1, lax.axis_size("ctx")):
        got = cross_to(low, "ctx", flip).astype(f32)
        spot = place ^ flip
        ahead = spot > place if backward else spot < place
        takes = jnp.logical_and(ahead, second(spot, end) == mine)
        received = received + jnp.where(takes, got, 0.0)
    received = yield received
    return received


def shards(tokens, lengths, gain_one, w_qkv, f_query, f_key, w_out, gain_two, w_up, w_down, d_out):
    rows, width = tokens.shape
    heads, size, _ = f_query.shape
    pairs = heads // 2
    wide = heads * size
    units = w_up.shape[1]
    assert size == 64 and lax.axis_size("heads") == 2 and 1536 % rows == 0
    boundary = lengths[0, 0]
    place = bit_of("ctx", 0)
    order = fetch_order()
    gain_one_row = gain_one.reshape(1, width)
    gain_two_row = gain_two.reshape(1, width)

    spots = np.arange(256) // 64
    ones = jnp.asarray(spots[:, None] == spots[None, :], bf16)
    cross = jnp.asarray((spots[:128, None] != spots[None, :128]) * (-1.0 / 64.0), bf16)
    signs = jnp.asarray(np.kron(np.array([[1, -1, 1, -1]]), np.eye(64)), bf16)

    flow = Flow()
    slot = flow.slot
    qkv_own = jnp.transpose(w_qkv, (1, 0, 2))
    maps_own = jnp.stack([f_query, f_key])
    flow.start("maps", send_once(maps_own, "heads", 0))
    flow.start("qkv", fetch_halves(qkv_own, 1))
    flow.start("up", fetch_quarters([w_up], ("ctx", 1), 1))
    flow.start("down", fetch_quarters([w_down, w_out], ("batch", 0), 0))
    (tokens,) = slot(["maps", "qkv"], (tokens,))

    h_one, turned_h = norm_one(tokens, gain_one_row)
    maps_oth = flow.done["maps"]
    keys = [key_pass(h_one, [qkv_own], order, maps_own, signs, [])]
    (keys[0][6], order, maps_oth, gain_two_row) = slot(
        ["qkv", "up", "down"], (keys[0][6], order, maps_oth, gain_two_row)
    )
    qkv_oth = flow.done["qkv"]
    keys.append(key_pass(h_one, qkv_oth, order, maps_oth, signs, [keys[0][6]]))
    flow.start("scan", scan_runs(keys[1][6], boundary, rows, False))
    (keys[1][1], order) = slot(["scan", "up"], (keys[1][1], order))
    queries = []
    for at, weights in enumerate(([qkv_own], qkv_oth)):
        queries.append(
            query_pass(
                h_one,
                weights,
                order,
                keys[at][4],
                keys[at][1],
                keys[at][5],
                (maps_own, maps_oth)[at],
                signs,
            )
        )
        if at == 0:
            (queries[0][0], order) = slot(["scan", "up", "down"], (queries[0][0], order))
    (queries[1][0], order) = slot(["scan", "down"], (queries[1][0], order))
    ups, downs, incoming = (flow.done[n] for n in ("up", "down", "scan"))
    q, phi_q, turned_pq, numer, _, fq = zip(*queries)
    k, v, turned_v, phi_k, turned_pk, prefix, _, _, fk = zip(*keys)

    attended, turned_a, inverse, resid, h_two, turned_two = front_pass(
        order, tokens, numer, phi_q, incoming, gain_two_row, w_out, downs, 512
    )
    send_up, send_down, keep_up, keep_down, *parts = feed_pass(
        order, h_two, turned_two, d_out, ups, downs, 768
    )
    flow.start("oth_up", send_over(send_up, keep_up))
    flow.start("oth_down", send_over_late(send_down, keep_down))
    slot(["oth_up", "oth_down"], ())
    (order,) = slot(["oth_up", "oth_down"], (order,))
    (
        act,
        grad_pre,
        mixed,
        grad_resid,
        gn,
        gd,
        turned_n,
        turned_gd,
        grad_totals,
    ) = middle_pass(
        order,
        resid,
        h_two,
        d_out,
        parts,
        attended,
        inverse,
        phi_q,
        gain_two_row,
        cross,
        (w_out, w_up, w_down),
        downs,
        incoming.shape,
        256,
        768,
    )
    flow.start("later", scan_runs(grad_totals, boundary, rows, True))
    near, away = place.reshape(1), (1 - place).reshape(1)
    (near, grad_pre) = slot(["later", "oth_up", "oth_down"], (near, grad_pre))
    up_sum = up_pass(near, turned_two, grad_pre, flow.done["oth_up"])
    (away, act, up_sum) = slot(["later", "oth_down"], (away, act, up_sum))
    everyone = ("batch", "ctx")
    up_sum = lax.psum_scatter(up_sum, everyone, scatter_dimension=0, tiled=True)
    send, out_send = down_pass(away, act, d_out, turned_a, grad_resid)
    flow.start("own_down", send_once(send, "ctx", 0))
    (near, out_send) = slot(["later", "own_down", "oth_down"], (near, out_send))
    keep_down, out_keep = down_pass(near, act, d_out, turned_a, grad_resid)
    got, right = flow.done["own_down"], flow.done["oth_down"]
    flow.start("down_sum", reduce_tail(keep_down, [got, right], 1))
    (near, out_keep) = slot(["down_sum"], (near, out_keep))
    later = flow.done["later"]

    grads, maps, sends, keeps = [[], []], [], [], []
    feeds = ["down_sum"]
    plan = [feeds, ["qkv0"] + feeds, ["qkv1", "qkv0"] + feeds]
    names = (q, k, v, turned_v, phi_q, turned_pq, phi_k, turned_pk)
    for at in range(pairs):
        own, oth, send, keep, map_part = back_pass(
            at,
            near,
            [[a[side] for a in names] for side in range(2)],
            [gn, gd, turned_n, turned_gd],
            prefix,
            incoming,
            later,
            fq,
            fk,
            ones,
            turned_h,
            maps if at == pairs - 1 else [],
        )
        grads[0].append(own)
        grads[1].append(oth)
        maps.append(map_part)
        sends.append(send)
        keeps.append(keep)
        if at == pairs - 2:
            flow.start(
                "qkv0",
                reduce_sums(
                    jnp.concatenate(sends + [out_send], axis=1),
                    jnp.concatenate(keeps + [out_keep], axis=1),
                    2,
                ),
            )
        if at == pairs - 1:
            flow.start("qkv1", reduce_sums(send, keep, 2))
        tied = (own, near) if at < pairs - 1 else (own, near, up_sum)
        (grads[0][at], near, *rest) = slot(plan[at], tied)
        if rest:
            (up_sum,) = rest
            up_sum = lax.all_gather(up_sum, everyone, axis=0, tiled=True)
    order = order + 0 * near[0]
    tokens_args = (tokens, grad_resid, gain_one_row, qkv_own, qkv_oth, grads[0] + grads[1], 256)
    blocks = rows // 256
    early = blocks // 2
    grad_tokens = tokens_pass(order, *tokens_args, 0, early)
    tail = ["qkv1", "qkv0"]
    (grad_tokens, order) = slot(tail + feeds, (grad_tokens, order))
    grad_tokens = tokens_pass(order, *tokens_args, early, blocks - early, grad_tokens)
    (grad_tokens,) = slot(tail + feeds, (grad_tokens,))
    (up_sum,) = slot(tail + feeds, (up_sum,))
    grad_up = up_sum.astype(f32)
    gain_two_part = jnp.sum(grad_up * w_up.astype(f32), axis=1)
    (grad_up, gain_two_part) = slot(tail + feeds, (grad_up, gain_two_part))
    flow.finish(feeds)
    grad_down = ordered(place, *flow.done["down_sum"]).astype(f32)
    (grad_down,) = slot(tail, (grad_down,))
    flow.finish(list(flow.steps))
    part = width // 2
    (mine, theirs), (mine_last, theirs_last) = flow.done["qkv0"], flow.done["qkv1"]
    join = lambda mine, theirs: ordered(place, mine, theirs)
    beside = lambda a: jnp.concatenate([a[: wide // 2], a[wide // 2 :]], axis=1)
    more = part * (pairs - 1)
    grad_out = join(beside(mine[more:]), beside(theirs[more:])).astype(f32)
    parts = [
        join(mine[part * at : part * at + part], theirs[part * at : part * at + part])
        for at in range(pairs - 1)
    ]
    parts.append(join(mine_last[:part], theirs_last[:part]))
    grad_qkv = jnp.stack(
        [
            jnp.concatenate([p[:, 128 * kind : 128 * kind + 128] for p in parts], axis=1)
            for kind in range(3)
        ]
    )
    grad_qkv = grad_qkv.astype(f32)
    gain_one_part = jnp.sum(grad_qkv * qkv_own.astype(f32), axis=(0, 2))
    gains = jnp.stack([gain_one_part, gain_two_part])
    gains = (gains + swap(gains, "heads", 0)) / jnp.stack([gain_one, gain_two])
    grad_qkv = jnp.transpose(grad_qkv, (1, 0, 2))
    maps_sum = join(mine_last[part : part + 64], theirs_last[part : part + 64]).astype(f32)
    maps_sum = maps_sum.reshape(2, 64, pairs, 2, 64).transpose(3, 2, 0, 1, 4)
    grad_maps = maps_sum.reshape(2, heads, size, size)
    return (
        mixed,
        grad_tokens,
        gains[0],
        grad_qkv,
        grad_maps[0],
        grad_maps[1],
        grad_out,
        gains[1],
        grad_up,
        grad_down,
    )


def solution(mesh):
    in_specs = (
        P(("batch", "ctx", "heads"), None),
        P("batch", None),
        P(),
        P(None, None, "heads"),
        P("heads", None, None),
        P("heads", None, None),
        P("heads", None),
        P(),
        P(None, "heads"),
        P("heads", None),
        P(("batch", "ctx", "heads"), None),
    )
    out_specs = (
        P(("batch", "ctx", "heads"), None),
        P(("batch", "ctx", "heads"), None),
        P(),
        P(None, None, "heads"),
        P("heads", None, None),
        P("heads", None, None),
        P("heads", None),
        P(),
        P(None, "heads"),
        P("heads", None),
    )
    return jax.shard_map(shards, mesh=mesh, in_specs=in_specs, out_specs=out_specs, check_vma=False)
```

profile of v0, /device:TPU:0, one launch (start us, length us, event | category | flops | bytes accessed | tf_op | source)
XLA Modules:
  0.0 394.5 jit_solution(10243082524725328245)
XLA Ops:
  8.6 3.0 collective-permute-start
  12.9 5.2 %norm_one.1 = (bf16[1536,768]{1,0:T(8,128)(2,1)}, bf16[768,1536]{1,0:T(8,128)(2,1)}) custom-call(bf16[1536,768]{1,0:T(8,128)(2,1)} %refs_1_.1, f32[1,768]{1,0:T(1,128)} %reshape.68.gain.refs_3_), custom_call_target="tpu_custom_call" | custom-call | bytes 18000000 | tf_op jit(solution)/shard_map/norm_one/pallas_call | solution.py:140
  18.8 10.4 %key_pass.2 = (bf16[384,1536]{1,0:T(8,128)(2,1)}, bf16[1536,384]{1,0:T(8,128)(2,1)}, bf16[384,1536]{1,0:T(8,128)(2,1)}, bf16[1536,768]{1,0:T(8,128)(2,1)}, bf16[...) custom-call(s32[10]{0:T(128)} %stack.81.order.refs_0_, ...), custom_call_target="tpu_custom_call" | custom-call | bytes 36000000 | tf_op jit(solution)/shard_map/key_pass/pallas_call | solution.py:228
  31.3 1.9 constant_dynamic-slice_fusion.2
  33.2 2.3 collective-permute-done.1.f
  35.6 1.8 collective-permute-start.3
  38.9 10.5 %key_pass.3 = (bf16[384,1536]{1,0:T(8,128)(2,1)}, bf16[1536,384]{1,0:T(8,128)(2,1)}, bf16[384,1536]{1,0:T(8,128)(2,1)}, bf16[1536,768]{1,0:T(8,128)(2,1)}, bf16[...) custom-call(s32[10]{0:T(128)} %stack.81.order.refs_0_, ...), custom_call_target="tpu_custom_call" | custom-call | bytes 36000000 | tf_op jit(solution)/shard_map/key_pass/pallas_call | solution.py:228
  49.4 2.7 collective-permute-done.3.refs_0_
  52.1 1.8 collective-permute-start.5
  55.5 15.2 %query_pass.2 = (bf16[384,1536]{1,0:T(8,128)(2,1)}, bf16[1536,768]{1,0:T(8,128)(2,1)}, bf16[768,1536]{1,0:T(8,128)(2,1)}, bf16[1536,768]{1,0:T(8,128)(2,1)}, bf1...) custom-call(s32[10]{0:T(128)} %stack.81.order.refs_0_, bf16[1536,768]{1,0:T(8,128)(2,1)} %get-tuple-element.177.h, ...), custom_call_target="tpu_custom_call" | custom-call | bytes 54000000 | tf_op jit(solution)/shard_map/query_pass/pallas_call | solution.py:320
  75.3 1.8 collective-permute-start.11
  77.1 1.6 collective-permute-start.10
  79.4 15.4 %query_pass.3 = (bf16[384,1536]{1,0:T(8,128)(2,1)}, bf16[1536,768]{1,0:T(8,128)(2,1)}, bf16[768,1536]{1,0:T(8,128)(2,1)}, bf16[1536,768]{1,0:T(8,128)(2,1)}, bf1...) custom-call(s32[10]{0:T(128)} %stack.81.order.refs_0_, bf16[1536,768]{1,0:T(8,128)(2,1)} %get-tuple-element.177.h, ...), custom_call_target="tpu_custom_call" | custom-call | bytes 54000000 | tf_op jit(solution)/shard_map/query_pass/pallas_call | solution.py:320
  94.9 2.0 select_add_fusion.1.refs_4_.refs_30_
  97.5 1.7 collective-permute-done.13.refs_10_.refs_7_.refs_14_
  100.1 13.0 %front_pass.1 = (bf16[1536,768]{1,0:T(8,128)(2,1)}, bf16[768,1536]{1,0:T(8,128)(2,1)}, bf16[1536,768]{1,0:T(8,128)(2,1)}, bf16[1536,768]{1,0:T(8,128)(2,1)}, bf1...) custom-call(s32[10]{0:T(128)} %stack.81.order.refs_0_, bf16[1536,768]{1,0:T(8,128)(2,1)} %refs_1_.1, ...), custom_call_target="tpu_custom_call" | custom-call | bytes 46800000 | tf_op jit(solution)/shard_map/front_pass/pallas_call | solution.py:440
  113.2 31.5 %feed_pass.1 = (bf16[768,768]{1,0:T(8,128)(2,1)}, bf16[768,768]{1,0:T(8,128)(2,1)}, bf16[768,768]{1,0:T(8,128)(2,1)}, bf16[768,768]{1,0:T(8,128)(2,1)}, bf16[153...) custom-call(s32[10]{0:T(128)} %stack.81.order.refs_0_, bf16[1536,768]{1,0:T(8,128)(2,1)} %get-tuple-element.212.h_any.h, ...), custom_call_target="tpu_custom_call" | custom-call | bytes 115200000 | tf_op jit(solution)/shard_map/feed_pass/pallas_call | solution.py:623
  145.3 2.5 collective-permute-done.16
  147.8 1.7 add_convert_fusion.5
  151.9 34.1 %middle_pass.1 = (bf16[1536,1536]{1,0:T(8,128)(2,1)}, bf16[2,1536,768]{2,1,0:T(8,128)(2,1)}, bf16[1536,768]{1,0:T(8,128)(2,1)}, bf16[1536,768]{1,0:T(8,128)(2,1)...) custom-call(s32[10]{0:T(128)} %stack.81.order.refs_0_, ...), custom_call_target="tpu_custom_call" | custom-call | bytes 126000000 | tf_op jit(solution)/shard_map/middle_pass/pallas_call | solution.py:755
  186.1 4.6 %collective-permute-done.18 = bf16[384,768]{1,0:T(8,128)(2,1)S(1)} collective-permute-done((bf16[384,768]{1,0:T(8,128)(2,1)S(1)}, bf16[384,768]{1,0:T(8,128)(2,1)S(1)}, u32[]{:S(2)}, u32[]{:S(2)}) %collective-permute-start.18) | collective-permute-done | bytes 589856 | tf_op jit(solution)/shard_map/ppermute | solution.py:1062
  192.1 8.1 %up_pass.1 = bf16[768,1536]{1,0:T(8,128)(2,1)} custom-call(s32[1]{0:T(128)} %bitcast.4.core, bf16[768,1536]{1,0:T(8,128)(2,1)} %get-tuple-element.213.turned_any.left, bf16[2,1536,768]{2,1,0:T(8,128)(2,1)} %get-tuple-element.239.right, bf16[768,768]{1,0:T(8,128)(2,1)} %copy-done.15), custom_call_target="tpu_custom_call" | custom-call | bytes 28800000 | tf_op jit(solution)/shard_map/up_pass/pallas_call | solution.py:801
  203.4 7.4 %down_pass.2 = (bf16[768,768]{1,0:T(8,128)(2,1)}, bf16[2,384,384]{2,1,0:T(8,128)(2,1)}) custom-call(s32[1]{0:T(128)} %bitcast.5.core, bf16[1536,1536]{1,0:T(8,128)(2,1)} %get-tuple-element.243.left, bf16[1536,768]{1,0:T(8,128)(2,1)} %right.3, bf16[768,1536]{1,0:T(8,128)(2,1)} %get-tuple-element.244.own_left.oth_left, ...), custom_call_target="tpu_custom_call" | custom-call | bytes 28800000 | tf_op jit(solution)/shard_map/down_pass/pallas_call | solution.py:833
  210.9 2.0 collective-permute-done.22
  215.7 7.5 %down_pass.3 = (bf16[768,768]{1,0:T(8,128)(2,1)}, bf16[2,384,384]{2,1,0:T(8,128)(2,1)}) custom-call(s32[1]{0:T(128)} %bitcast.4.core, bf16[1536,1536]{1,0:T(8,128)(2,1)} %get-tuple-element.243.left, bf16[1536,768]{1,0:T(8,128)(2,1)} %right.3, bf16[768,1536]{1,0:T(8,128)(2,1)} %get-tuple-element.244.own_left.oth_left, ...), custom_call_target="tpu_custom_call" | custom-call | bytes 28800000 | tf_op jit(solution)/shard_map/down_pass/pallas_call | solution.py:833
  226.6 17.2 %back_pass.3 = (bf16[1536,384]{1,0:T(8,128)(2,1)}, bf16[1536,384]{1,0:T(8,128)(2,1)}, bf16[2,384,384]{2,1,0:T(8,128)(2,1)}, bf16[2,384,384]{2,1,0:T(8,128)(2,1)}, bf16[2,128,128]{2,1,0:T(8,128)(2,1)}) custom-call(s32[1]{0:T(128)} %bitcast.4.core, bf16[384,1536]{1,0:T(8,128)(2,1)} %get-tuple-element.256.refs_0_, ...), custom_call_target="tpu_custom_call" | custom-call | bytes 61200000 | tf_op jit(solution)/shard_map/back_pass/pallas_call | solution.py:968
  244.5 16.9 %back_pass.4 = (bf16[1536,384]{1,0:T(8,128)(2,1)}, bf16[1536,384]{1,0:T(8,128)(2,1)}, bf16[2,384,384]{2,1,0:T(8,128)(2,1)}, bf16[2,384,384]{2,1,0:T(8,128)(2,1)}, bf16[2,128,128]{2,1,0:T(8,128)(2,1)}) custom-call(s32[1]{0:T(128)} %bitcast.4.core, bf16[384,1536]{1,0:T(8,128)(2,1)} %get-tuple-element.256.refs_0_, ...), custom_call_target="tpu_custom_call" | custom-call | bytes 61200000 | tf_op jit(solution)/shard_map/back_pass/pallas_call | solution.py:968
  268.4 2.6 collective-permute-start.29
  271.0 17.6 %back_pass.5 = (bf16[1536,384]{1,0:T(8,128)(2,1)}, bf16[1536,384]{1,0:T(8,128)(2,1)}, bf16[2,512,384]{2,1,0:T(8,128)(2,1)}, bf16[2,512,384]{2,1,0:T(8,128)(2,1)}, bf16[2,128,128]{2,1,0:T(8,128)(2,1)}) custom-call(s32[1]{0:T(128)} %bitcast.4.core, bf16[384,1536]{1,0:T(8,128)(2,1)} %get-tuple-element.256.refs_0_, ...), custom_call_target="tpu_custom_call" | custom-call | bytes 61200000 | tf_op jit(solution)/shard_map/back_pass/pallas_call | solution.py:968
  290.6 1.8 collective-permute-done.30
  294.6 2.6 collective-permute-start.33
  297.2 9.2 %tokens_pass.2.refs_13_ = bf16[1536,768]{1,0:T(8,128)(2,1)} custom-call(s32[10]{0:T(128)} %stack.81.order.refs_0_, bf16[1536,768]{1,0:T(8,128)(2,1)} %refs_1_.1, bf16[1536,768]{1,0:T(8,128)(2,1)} %get-tuple-element.245.right_more.refs_2_, f32[1,768]{1,0:T(1,128)} %reshape.68.gain.refs_3_, bf16[3,768,384]{2,1,0:T(8,128)(2,1)} %bitcast.47, ...), custom_call_target="tpu_custom_call" | custom-call | bytes 28800000 | tf_op jit(solution)/shard_map/tokens_pass/pallas_call | solution.py:1037
  306.8 1.9 collective-permute-start.35
  308.7 3.4 collective-permute-start.36
  313.2 9.3 %tokens_pass.3 = bf16[1536,768]{1,0:T(8,128)(2,1)} custom-call(s32[10]{0:T(128)} %stack.81.order.refs_0_, bf16[1536,768]{1,0:T(8,128)(2,1)} %refs_1_.1, bf16[1536,768]{1,0:T(8,128)(2,1)} %get-tuple-element.245.right_more.refs_2_, f32[1,768]{1,0:T(1,128)} %reshape.68.gain.refs_3_, bf16[3,768,384]{2,1,0:T(8,128)(2,1)} %bitcast.48, ...), custom_call_target="tpu_custom_call", output_to_operand_aliasing={{}: (13, {})} | custom-call | bytes 28800000 | tf_op jit(solution)/shard_map/tokens_pass/pallas_call | solution.py:1037
  322.7 7.1 %collective-permute-done.38 = bf16[192,768]{1,0:T(8,128)(2,1)S(1)} collective-permute-done((bf16[192,768]{1,0:T(8,128)(2,1)S(1)}, bf16[192,768]{1,0:T(8,128)(2,1)S(1)}, u32[]{:S(2)}, u32[]{:S(2)}) %collective-permute-start.38) | collective-permute-done | bytes 294944 | tf_op jit(solution)/shard_map/ppermute | solution.py:1062
  330.0 2.5 collective-permute-start.39
  332.5 5.4 %collective-permute-start.40 = (bf16[64,384]{1,0:T(8,128)(2,1)S(1)}, bf16[64,384]{1,0:T(8,128)(2,1)S(1)}, u32[]{:S(2)}, u32[]{:S(2)}) collective-permute-start(bf16[64,384]{1,0:T(8,128)(2,1)S(1)} %get-tuple-element.321), channel_id=1, source_target_pairs={{0,16},{8,24},{16,0},{24,8},{1,17},{9,25},{17,1},{25,9},{2,18},{10... | collective-permute-start | bytes 147464 | tf_op jit(solution)/shard_map/ppermute | solution.py:1062
  338.9 3.8 collective-permute-start.43
  345.2 4.8 %collective-permute-done.43 = bf16[144,384]{1,0:T(8,128)(2,1)S(1)} collective-permute-done((bf16[144,384]{1,0:T(8,128)(2,1)S(1)}, bf16[144,384]{1,0:T(8,128)(2,1)S(1)}, u32[]{:S(2)}, u32[]{:S(2)}) %collective-permute-start.43) | collective-permute-done | bytes 110624 | tf_op jit(solution)/shard_map/ppermute | solution.py:1062
  351.1 2.0 maximum_select_fusion.1
  355.6 2.5 multiply_reduce_fusion
  358.2 2.8 convert_element_type.465
  362.2 1.7 collective-permute-start.48
  363.9 3.6 collective-permute-done.47
  369.6 1.7 collective-permute-start.51
  371.3 4.4 %fusion.1 = f32[1536,768]{1,0:T(8,128)} fusion(bf16[768,768]{1,0:T(8,128)(2,1)} %copy-done.12, bf16[768,768]{1,0:T(8,128)(2,1)S(1)} %maximum_select_fusion.1, pred[]{:T(512)S(6)} %eq.68), kind=kLoop, calls=%fused_computation.5 | loop fusion | flops 11796480 | bytes 7077889 | tf_op jit(solution)/shard_map/convert_element_type | solution.py:1403
  383.4 2.1 convert_bitcast_fusion
  (241 shorter events, 62.0 us)
Async XLA Ops:
  7.2 282.6 %reduce-scatter.2.cloned.1.call-start = ((), (), s32[]{:S(2)}) async-start(), calls=%async_computation.1 | async-start | bytes 2506752 | tf_op jit(solution)/shard_map/reduce_scatter | solution.py:1339
  8.6 26.9 %collective-permute-start = (bf16[3,384,384]{2,1,0:T(8,128)(2,1)S(1)}, bf16[3,384,384]{2,1,0:T(8,128)(2,1)S(1)}, u32[]{:S(2)}, u32[]{:S(2)}) collective-permute-start(bf16[3,384,384]{2,1,0:T(8,128)(2,1)S(1)} %dynamic-slice_bitcast_fusion), channel_id=1, source_target_pairs={{0,1},{1,0},{2,3},{3,2},{4,5},{5,4},{6,7},{7,6},{8,9},{9,8},{10,11... | collective-permute-start | bytes 2654216 | tf_op jit(solution)/shard_map/ppermute | solution.py:1062
  11.7 23.9 %collective-permute-start.1 = (bf16[2,6,64,64]{3,2,1,0:T(8,128)(2,1)S(1)}, bf16[2,6,64,64]{3,2,1,0:T(8,128)(2,1)S(1)}, u32[]{:S(2)}, u32[]{:S(2)}) collective-permute-start(bf16[2,6,64,64]{3,2,1,0:T(8,128)(2,1)S(1)} %pad_maximum_fusion.3.f), channel_id=1, source_target_pairs={{0,1},{1,0},{2,3},{3,2},{4,5},{5,4},{6,7},{7,6},{8,9},{9,8},{10,11... | collective-permute-start | bytes 294920 | tf_op jit(solution)/shard_map/ppermute | solution.py:1062
  35.6 16.5 %collective-permute-start.3 = (bf16[768,384]{1,0:T(8,128)(2,1)}, bf16[768,384]{1,0:T(8,128)(2,1)}, u32[]{:S(2)}, u32[]{:S(2)}) collective-permute-start(bf16[768,384]{1,0:T(8,128)(2,1)} %constant_dynamic-slice_fusion.2), channel_id=1, source_target_pairs={{0,1},{1,0},{2,3},{3,2},{4,5},{5,4},{6,7},{7,6},{8,9},{9,8},{10,11... | collective-permute-start | bytes 1769480 | tf_op jit(solution)/shard_map/ppermute | solution.py:1062
  37.4 36.2 %collective-permute-start.7 = (bf16[480,768]{1,0:T(8,128)(2,1)S(1)}, bf16[480,768]{1,0:T(8,128)(2,1)S(1)}, u32[]{:S(2)}, u32[]{:S(2)}) collective-permute-start(bf16[480,768]{1,0:T(8,128)(2,1)S(1)} %pad_maximum_fusion.2), channel_id=1, source_target_pairs={{0,1},{1,0},{2,3},{3,2},{4,5},{5,4},{6,7},{7,6},{8,9},{9,8},{10,11... | collective-permute-start | bytes 2211848 | tf_op jit(solution)/shard_map/ppermute | solution.py:1062
  52.1 21.5 %collective-permute-start.5 = (bf16[768,384]{1,0:T(8,128)(2,1)}, bf16[768,384]{1,0:T(8,128)(2,1)S(1)}, u32[]{:S(2)}, u32[]{:S(2)}) collective-permute-start(bf16[768,384]{1,0:T(8,128)(2,1)} %collective-permute-done.3.refs_0_), channel_id=1, source_target_pairs={{0,4},{2,6},{4,0},{6,2},{1,5},{3,7},{5,1},{7,3},{8,12},{10,14},{12... | collective-permute-start | bytes 1769480 | tf_op jit(solution)/shard_map/ppermute | solution.py:1062
  53.9 19.7 %collective-permute-start.6 = (bf16[768,384]{1,0:T(8,128)(2,1)}, bf16[768,384]{1,0:T(8,128)(2,1)S(1)}, u32[]{:S(2)}, u32[]{:S(2)}) collective-permute-start(bf16[768,384]{1,0:T(8,128)(2,1)} %collective-permute-done.3.refs_0_), channel_id=1, source_target_pairs={{0,2},{2,0},{4,6},{6,4},{1,3},{3,1},{5,7},{7,5},{8,10},{10,8},{12,... | collective-permute-start | bytes 1769480 | tf_op jit(solution)/shard_map/ppermute | solution.py:1062
  53.9 18.0 %collective-permute-start.4 = (bf16[2,400,128]{2,1,0:T(8,128)(2,1)}, bf16[2,400,128]{2,1,0:T(8,128)(2,1)}, u32[]{:S(2)}, u32[]{:S(2)}) collective-permute-start(bf16[2,400,128]{2,1,0:T(8,128)(2,1)} %get-tuple-element.187), channel_id=1, source_target_pairs={{0,1},{1,0},{2,3},{3,2},{4,5},{5,4},{6,7},{7,6},{8,9},{9,8},{10,11... | collective-permute-start | bytes 614408 | tf_op jit(solution)/shard_map/ppermute | solution.py:1062
  75.3 21.6 %collective-permute-start.11 = (bf16[480,768]{1,0:T(8,128)(2,1)S(1)}, bf16[480,768]{1,0:T(8,128)(2,1)S(1)}, u32[]{:S(2)}, u32[]{:S(2)}) collective-permute-start(bf16[480,768]{1,0:T(8,128)(2,1)S(1)} %collective-permute-done.7.refs_7_.refs_4_.refs_11_), channel_id=1, source_target_pairs={{0,8},{8,0},{16,24},{24,16},{1,9},{9,1},{17,25},{25,17},{2,10},{10... | collective-permute-start | bytes 2211848 | tf_op jit(solution)/shard_map/ppermute | solution.py:1062
  77.1 19.8 %collective-permute-start.12 = (bf16[480,768]{1,0:T(8,128)(2,1)S(1)}, bf16[480,768]{1,0:T(8,128)(2,1)S(1)}, u32[]{:S(2)}, u32[]{:S(2)}) collective-permute-start(bf16[480,768]{1,0:T(8,128)(2,1)S(1)} %collective-permute-done.7.refs_7_.refs_4_.refs_11_), channel_id=1, source_target_pairs={{0,2},{2,0},{4,6},{6,4},{1,3},{3,1},{5,7},{7,5},{8,10},{10,8},{12,... | collective-permute-start | bytes 2211848 | tf_op jit(solution)/shard_map/ppermute | solution.py:1062
  77.1 17.8 %collective-permute-start.10 = (bf16[2,400,128]{2,1,0:T(8,128)(2,1)}, bf16[2,400,128]{2,1,0:T(8,128)(2,1)S(1)}, u32[]{:S(2)}, u32[]{:S(2)}) collective-permute-start(bf16[2,400,128]{2,1,0:T(8,128)(2,1)} %fusion.7), channel_id=1, source_target_pairs={{0,6},{2,4},{4,2},{6,0},{1,7},{3,5},{5,3},{7,1},{8,14},{10,12},{12... | collective-permute-start | bytes 614408 | tf_op jit(solution)/shard_map/ppermute | solution.py:1062
  78.8 16.2 %collective-permute-start.8 = (bf16[2,400,128]{2,1,0:T(8,128)(2,1)}, bf16[2,400,128]{2,1,0:T(8,128)(2,1)}, u32[]{:S(2)}, u32[]{:S(2)}) collective-permute-start(bf16[2,400,128]{2,1,0:T(8,128)(2,1)} %fusion.7), channel_id=1, source_target_pairs={{0,2},{2,0},{4,6},{6,4},{1,3},{3,1},{5,7},{7,5},{8,10},{10,8},{12,... | collective-permute-start | bytes 614408 | tf_op jit(solution)/shard_map/ppermute | solution.py:1062
  78.8 16.2 %collective-permute-start.9 = (bf16[2,400,128]{2,1,0:T(8,128)(2,1)}, bf16[2,400,128]{2,1,0:T(8,128)(2,1)}, u32[]{:S(2)}, u32[]{:S(2)}) collective-permute-start(bf16[2,400,128]{2,1,0:T(8,128)(2,1)} %fusion.7), channel_id=1, source_target_pairs={{0,4},{2,6},{4,0},{6,2},{1,5},{3,7},{5,1},{7,3},{8,12},{10,14},{12... | collective-permute-start | bytes 614408 | tf_op jit(solution)/shard_map/ppermute | solution.py:1062
  97.2 15.9 %collective-permute-start.14 = (bf16[768,384]{1,0:T(8,128)(2,1)S(1)}, bf16[768,384]{1,0:T(8,128)(2,1)}, u32[]{:S(2)}, u32[]{:S(2)}) collective-permute-start(bf16[768,384]{1,0:T(8,128)(2,1)S(1)} %copy-done.19), channel_id=1, source_target_pairs={{0,2},{2,0},{4,6},{6,4},{1,3},{3,1},{5,7},{7,5},{8,10},{10,8},{12,... | collective-permute-start | bytes 1769480 | tf_op jit(solution)/shard_map/ppermute | solution.py:1062
  149.8 40.8 %collective-permute-start.17 = (bf16[768,768]{1,0:T(8,128)(2,1)S(1)}, bf16[768,768]{1,0:T(8,128)(2,1)S(1)}, u32[]{:S(2)}, u32[]{:S(2)}) collective-permute-start(bf16[768,768]{1,0:T(8,128)(2,1)S(1)} %add_convert_fusion), channel_id=1, source_target_pairs={{0,1},{1,0},{2,3},{3,2},{4,5},{5,4},{6,7},{7,6},{8,9},{9,8},{10,11... | collective-permute-start | bytes 3538952 | tf_op jit(solution)/shard_map/ppermute | solution.py:1062
  151.4 39.2 %collective-permute-start.18 = (bf16[384,768]{1,0:T(8,128)(2,1)S(1)}, bf16[384,768]{1,0:T(8,128)(2,1)S(1)}, u32[]{:S(2)}, u32[]{:S(2)}) collective-permute-start(bf16[384,768]{1,0:T(8,128)(2,1)S(1)} %get-tuple-element.232), channel_id=1, source_target_pairs={{0,1},{1,0},{2,3},{3,2},{4,5},{5,4},{6,7},{7,6},{8,9},{9,8},{10,11... | collective-permute-start | bytes 1769480 | tf_op jit(solution)/shard_map/ppermute | solution.py:1062
  190.6 9.6 %collective-permute-start.19 = (bf16[2,400,128]{2,1,0:T(8,128)(2,1)}, bf16[2,400,128]{2,1,0:T(8,128)(2,1)S(1)}, u32[]{:S(2)}, u32[]{:S(2)}) collective-permute-start(bf16[2,400,128]{2,1,0:T(8,128)(2,1)} %get-tuple-element.235), channel_id=1, source_target_pairs={{0,1},{1,0},{2,3},{3,2},{4,5},{5,4},{6,7},{7,6},{8,9},{9,8},{10,11... | collective-permute-start | bytes 614408 | tf_op jit(solution)/shard_map/ppermute | solution.py:1062
  200.3 14.4 %collective-permute-start.23 = (bf16[384,768]{1,0:T(8,128)(2,1)S(1)}, bf16[384,768]{1,0:T(8,128)(2,1)S(1)}, u32[]{:S(2)}, u32[]{:S(2)}) collective-permute-start(bf16[384,768]{1,0:T(8,128)(2,1)S(1)} %get-tuple-element.247), channel_id=1, source_target_pairs={{0,1},{1,0},{2,3},{3,2},{4,5},{5,4},{6,7},{7,6},{8,9},{9,8},{10,11... | collective-permute-start | bytes 1769480 | tf_op jit(solution)/shard_map/ppermute | solution.py:1062
  201.4 9.4 %collective-permute-start.20 = (bf16[2,400,128]{2,1,0:T(8,128)(2,1)S(1)}, bf16[2,400,128]{2,1,0:T(8,128)(2,1)S(1)}, u32[]{:S(2)}, u32[]{:S(2)}) collective-permute-start(bf16[2,400,128]{2,1,0:T(8,128)(2,1)S(1)} %fusion.10), channel_id=1, source_target_pairs={{0,2},{2,0},{4,6},{6,4},{1,3},{3,1},{5,7},{7,5},{8,10},{10,8},{12,... | collective-permute-start | bytes 614408 | tf_op jit(solution)/shard_map/ppermute | solution.py:1062
  201.4 9.4 %collective-permute-start.21 = (bf16[2,400,128]{2,1,0:T(8,128)(2,1)S(1)}, bf16[2,400,128]{2,1,0:T(8,128)(2,1)S(1)}, u32[]{:S(2)}, u32[]{:S(2)}) collective-permute-start(bf16[2,400,128]{2,1,0:T(8,128)(2,1)S(1)} %fusion.10), channel_id=1, source_target_pairs={{0,4},{2,6},{4,0},{6,2},{1,5},{3,7},{5,1},{7,3},{8,12},{10,14},{12... | collective-permute-start | bytes 614408 | tf_op jit(solution)/shard_map/ppermute | solution.py:1062
  202.9 10.0 %collective-permute-start.22 = (bf16[2,400,128]{2,1,0:T(8,128)(2,1)S(1)}, bf16[2,400,128]{2,1,0:T(8,128)(2,1)S(1)}, u32[]{:S(2)}, u32[]{:S(2)}) collective-permute-start(bf16[2,400,128]{2,1,0:T(8,128)(2,1)S(1)} %fusion.10), channel_id=1, source_target_pairs={{0,6},{2,4},{4,2},{6,0},{1,7},{3,5},{5,3},{7,1},{8,14},{10,12},{12... | collective-permute-start | bytes 614408 | tf_op jit(solution)/shard_map/ppermute | solution.py:1062
  215.6 7.6 %collective-permute-start.24 = (bf16[768,768]{1,0:T(8,128)(2,1)}, bf16[768,768]{1,0:T(8,128)(2,1)S(1)}, u32[]{:S(2)}, u32[]{:S(2)}) collective-permute-start(bf16[768,768]{1,0:T(8,128)(2,1)} %get-tuple-element.251), channel_id=1, source_target_pairs={{0,2},{2,0},{4,6},{6,4},{1,3},{3,1},{5,7},{7,5},{8,10},{10,8},{12,... | collective-permute-start | bytes 3538952 | tf_op jit(solution)/shard_map/ppermute | solution.py:1062
  224.9 18.9 %collective-permute-start.25 = (bf16[384,768]{1,0:T(8,128)(2,1)S(1)}, bf16[384,768]{1,0:T(8,128)(2,1)S(1)}, u32[]{:S(2)}, u32[]{:S(2)}) collective-permute-start(bf16[384,768]{1,0:T(8,128)(2,1)S(1)} %get-tuple-element.278), channel_id=1, source_target_pairs={{0,4},{2,6},{4,0},{6,2},{1,5},{3,7},{5,1},{7,3},{8,12},{10,14},{12... | collective-permute-start | bytes 1769480 | tf_op jit(solution)/shard_map/ppermute | solution.py:1062
  226.5 126.6 %all-gather.2.cloned.1.call-start = ((), (), s32[]{:S(2)}) async-start(), calls=%async_computation.2 | async-start | bytes 2506752 | tf_op jit(solution)/shard_map/all_gather | solution.py:1388
  243.9 18.8 %collective-permute-start.26 = (bf16[192,768]{1,0:T(8,128)(2,1)S(1)}, bf16[192,768]{1,0:T(8,128)(2,1)S(1)}, u32[]{:S(2)}, u32[]{:S(2)}) collective-permute-start(bf16[192,768]{1,0:T(8,128)(2,1)S(1)} %get-tuple-element.284), channel_id=1, source_target_pairs={{0,8},{8,0},{16,24},{24,16},{1,9},{9,1},{17,25},{25,17},{2,10},{10... | collective-permute-start | bytes 884744 | tf_op jit(solution)/shard_map/ppermute | solution.py:1062
  267.1 21.8 %collective-permute-start.28 = (bf16[1152,384]{1,0:T(8,128)(2,1)S(1)}, bf16[1152,384]{1,0:T(8,128)(2,1)S(1)}, u32[]{:S(2)}, u32[]{:S(2)}) collective-permute-start(bf16[1152,384]{1,0:T(8,128)(2,1)S(1)} %get-tuple-element.343), channel_id=1, source_target_pairs={{0,1},{1,0},{2,3},{3,2},{4,5},{5,4},{6,7},{7,6},{8,9},{9,8},{10,11... | collective-permute-start | bytes 2654216 | tf_op jit(solution)/shard_map/ppermute | solution.py:1062
  268.4 20.2 %collective-permute-start.29 = (bf16[96,768]{1,0:T(8,128)(2,1)S(1)}, bf16[96,768]{1,0:T(8,128)(2,1)S(1)}, u32[]{:S(2)}, u32[]{:S(2)}) collective-permute-start(bf16[96,768]{1,0:T(8,128)(2,1)S(1)} %get-tuple-element.296), channel_id=1, source_target_pairs={{0,16},{8,24},{16,0},{24,8},{1,17},{9,25},{17,1},{25,9},{2,18},{10... | collective-permute-start | bytes 442376 | tf_op jit(solution)/shard_map/ppermute | solution.py:1062
  289.9 16.6 %collective-permute-start.32 = (bf16[576,384]{1,0:T(8,128)(2,1)}, bf16[576,384]{1,0:T(8,128)(2,1)S(1)}, u32[]{:S(2)}, u32[]{:S(2)}) collective-permute-start(bf16[576,384]{1,0:T(8,128)(2,1)} %get-tuple-element.301), channel_id=1, source_target_pairs={{0,4},{2,6},{4,0},{6,2},{1,5},{3,7},{5,1},{7,3},{8,12},{10,14},{12... | collective-permute-start | bytes 1327112 | tf_op jit(solution)/shard_map/ppermute | solution.py:1062
  293.3 13.3 %collective-permute-start.31 = (bf16[512,384]{1,0:T(8,128)(2,1)}, bf16[512,384]{1,0:T(8,128)(2,1)S(1)}, u32[]{:S(2)}, u32[]{:S(2)}) collective-permute-start(bf16[512,384]{1,0:T(8,128)(2,1)} %get-tuple-element.351), channel_id=1, source_target_pairs={{0,1},{1,0},{2,3},{3,2},{4,5},{5,4},{6,7},{7,6},{8,9},{9,8},{10,11... | collective-permute-start | bytes 1179656 | tf_op jit(solution)/shard_map/ppermute | solution.py:1062
  294.6 11.8 %collective-permute-start.33 = (bf16[96,768]{1,0:T(8,128)(2,1)S(1)}, bf16[96,768]{1,0:T(8,128)(2,1)S(1)}, u32[]{:S(2)}, u32[]{:S(2)}) collective-permute-start(bf16[96,768]{1,0:T(8,128)(2,1)S(1)} %add_convert_fusion.11), channel_id=1, source_target_pairs={{0,16},{8,24},{16,0},{24,8},{1,17},{9,25},{17,1},{25,9},{2,18},{10... | collective-permute-start | bytes 442376 | tf_op jit(solution)/shard_map/ppermute | solution.py:1062
  306.8 15.7 %collective-permute-start.35 = (bf16[144,384]{1,0:T(8,128)(2,1)S(1)}, bf16[144,384]{1,0:T(8,128)(2,1)S(1)}, u32[]{:S(2)}, u32[]{:S(2)}) collective-permute-start(bf16[144,384]{1,0:T(8,128)(2,1)S(1)} %get-tuple-element.312), channel_id=1, source_target_pairs={{0,8},{8,0},{16,24},{24,16},{1,9},{9,1},{17,25},{25,17},{2,10},{10... | collective-permute-start | bytes 331784 | tf_op jit(solution)/shard_map/ppermute | solution.py:1062
  308.7 13.8 %collective-permute-start.36 = (bf16[144,384]{1,0:T(8,128)(2,1)S(1)}, bf16[144,384]{1,0:T(8,128)(2,1)S(1)}, u32[]{:S(2)}, u32[]{:S(2)}) collective-permute-start(bf16[144,384]{1,0:T(8,128)(2,1)S(1)} %get-tuple-element.313), channel_id=1, source_target_pairs={{0,16},{8,24},{16,0},{24,8},{1,17},{9,25},{17,1},{25,9},{2,18},{10... | collective-permute-start | bytes 331784 | tf_op jit(solution)/shard_map/ppermute | solution.py:1062
  312.1 10.4 %collective-permute-start.37 = (bf16[144,384]{1,0:T(8,128)(2,1)S(1)}, bf16[144,384]{1,0:T(8,128)(2,1)S(1)}, u32[]{:S(2)}, u32[]{:S(2)}) collective-permute-start(bf16[144,384]{1,0:T(8,128)(2,1)S(1)} %get-tuple-element.314), channel_id=1, source_target_pairs={{0,24},{8,16},{16,8},{24,0},{1,25},{9,17},{17,9},{25,1},{2,26},{10... | collective-permute-start | bytes 331784 | tf_op jit(solution)/shard_map/ppermute | solution.py:1062
  312.1 17.6 %collective-permute-start.38 = (bf16[192,768]{1,0:T(8,128)(2,1)S(1)}, bf16[192,768]{1,0:T(8,128)(2,1)S(1)}, u32[]{:S(2)}, u32[]{:S(2)}) collective-permute-start(bf16[192,768]{1,0:T(8,128)(2,1)S(1)} %maximum_select_fusion.10), channel_id=1, source_target_pairs={{0,8},{8,0},{16,24},{24,16},{1,9},{9,1},{17,25},{25,17},{2,10},{10... | collective-permute-start | bytes 884744 | tf_op jit(solution)/shard_map/ppermute | solution.py:1062
  312.7 9.9 %collective-permute-start.34 = (bf16[256,384]{1,0:T(8,128)(2,1)S(1)}, bf16[256,384]{1,0:T(8,128)(2,1)S(1)}, u32[]{:S(2)}, u32[]{:S(2)}) collective-permute-start(bf16[256,384]{1,0:T(8,128)(2,1)S(1)} %get-tuple-element.310), channel_id=1, source_target_pairs={{0,4},{2,6},{4,0},{6,2},{1,5},{3,7},{5,1},{7,3},{8,12},{10,14},{12... | collective-permute-start | bytes 589832 | tf_op jit(solution)/shard_map/ppermute | solution.py:1062
  330.0 8.9 %collective-permute-start.39 = (bf16[64,384]{1,0:T(8,128)(2,1)S(1)}, bf16[64,384]{1,0:T(8,128)(2,1)S(1)}, u32[]{:S(2)}, u32[]{:S(2)}) collective-permute-start(bf16[64,384]{1,0:T(8,128)(2,1)S(1)} %get-tuple-element.320), channel_id=1, source_target_pairs={{0,8},{8,0},{16,24},{24,16},{1,9},{9,1},{17,25},{25,17},{2,10},{10... | collective-permute-start | bytes 147464 | tf_op jit(solution)/shard_map/ppermute | solution.py:1062
  332.5 10.2 %collective-permute-start.40 = (bf16[64,384]{1,0:T(8,128)(2,1)S(1)}, bf16[64,384]{1,0:T(8,128)(2,1)S(1)}, u32[]{:S(2)}, u32[]{:S(2)}) collective-permute-start(bf16[64,384]{1,0:T(8,128)(2,1)S(1)} %get-tuple-element.321), channel_id=1, source_target_pairs={{0,16},{8,24},{16,0},{24,8},{1,17},{9,25},{17,1},{25,9},{2,18},{10... | collective-permute-start | bytes 147464 | tf_op jit(solution)/shard_map/ppermute | solution.py:1062
  337.9 6.6 %collective-permute-start.41 = (bf16[64,384]{1,0:T(8,128)(2,1)S(1)}, bf16[64,384]{1,0:T(8,128)(2,1)S(1)}, u32[]{:S(2)}, u32[]{:S(2)}) collective-permute-start(bf16[64,384]{1,0:T(8,128)(2,1)S(1)} %get-tuple-element.322), channel_id=1, source_target_pairs={{0,24},{8,16},{16,8},{24,0},{1,25},{9,17},{17,9},{25,1},{2,26},{10... | collective-permute-start | bytes 147464 | tf_op jit(solution)/shard_map/ppermute | solution.py:1062
  337.9 13.2 %collective-permute-start.45 = (bf16[384,768]{1,0:T(8,128)(2,1)S(1)}, bf16[384,768]{1,0:T(8,128)(2,1)}, u32[]{:S(2)}, u32[]{:S(2)}) collective-permute-start(bf16[384,768]{1,0:T(8,128)(2,1)S(1)} %maximum_select_fusion.3), channel_id=1, source_target_pairs={{0,4},{2,6},{4,0},{6,2},{1,5},{3,7},{5,1},{7,3},{8,12},{10,14},{12... | collective-permute-start | bytes 1769480 | tf_op jit(solution)/shard_map/ppermute | solution.py:1062
  338.3 6.8 %collective-permute-start.42 = (bf16[144,384]{1,0:T(8,128)(2,1)S(1)}, bf16[144,384]{1,0:T(8,128)(2,1)S(1)}, u32[]{:S(2)}, u32[]{:S(2)}) collective-permute-start(bf16[144,384]{1,0:T(8,128)(2,1)S(1)} %add_convert_fusion.14), channel_id=1, source_target_pairs={{0,8},{8,0},{16,24},{24,16},{1,9},{9,1},{17,25},{25,17},{2,10},{10... | collective-permute-start | bytes 331784 | tf_op jit(solution)/shard_map/ppermute | solution.py:1062
  338.9 11.2 %collective-permute-start.43 = (bf16[144,384]{1,0:T(8,128)(2,1)S(1)}, bf16[144,384]{1,0:T(8,128)(2,1)S(1)}, u32[]{:S(2)}, u32[]{:S(2)}) collective-permute-start(bf16[144,384]{1,0:T(8,128)(2,1)S(1)} %add_convert_fusion.14), channel_id=1, source_target_pairs={{0,16},{8,24},{16,0},{24,8},{1,17},{9,25},{17,1},{25,9},{2,18},{10... | collective-permute-start | bytes 331784 | tf_op jit(solution)/shard_map/ppermute | solution.py:1062
  342.7 7.3 %collective-permute-start.44 = (bf16[144,384]{1,0:T(8,128)(2,1)S(1)}, bf16[144,384]{1,0:T(8,128)(2,1)S(1)}, u32[]{:S(2)}, u32[]{:S(2)}) collective-permute-start(bf16[144,384]{1,0:T(8,128)(2,1)S(1)} %add_convert_fusion.14), channel_id=1, source_target_pairs={{0,24},{8,16},{16,8},{24,0},{1,25},{9,17},{17,9},{25,1},{2,26},{10... | collective-permute-start | bytes 331784 | tf_op jit(solution)/shard_map/ppermute | solution.py:1062
  353.1 15.5 %collective-permute-start.50 = (bf16[768,768]{1,0:T(8,128)(2,1)S(1)}, bf16[768,768]{1,0:T(8,128)(2,1)S(1)}, u32[]{:S(2)}, u32[]{:S(2)}) collective-permute-start(bf16[768,768]{1,0:T(8,128)(2,1)S(1)} %maximum_select_fusion.1), channel_id=1, source_target_pairs={{0,2},{2,0},{4,6},{6,4},{1,3},{3,1},{5,7},{7,5},{8,10},{10,8},{12,... | collective-permute-start | bytes 3538952 | tf_op jit(solution)/shard_map/ppermute | solution.py:1062
  353.2 15.0 %collective-permute-start.49 = (bf16[576,384]{1,0:T(8,128)(2,1)}, bf16[576,384]{1,0:T(8,128)(2,1)S(1)}, u32[]{:S(2)}, u32[]{:S(2)}) collective-permute-start(bf16[576,384]{1,0:T(8,128)(2,1)} %maximum_select_fusion.8), channel_id=1, source_target_pairs={{0,4},{2,6},{4,0},{6,2},{1,5},{3,7},{5,1},{7,3},{8,12},{10,14},{12... | collective-permute-start | bytes 1327112 | tf_op jit(solution)/shard_map/ppermute | solution.py:1062
  354.1 9.8 %collective-permute-start.46 = (bf16[64,384]{1,0:T(8,128)(2,1)}, bf16[64,384]{1,0:T(8,128)(2,1)S(1)}, u32[]{:S(2)}, u32[]{:S(2)}) collective-permute-start(bf16[64,384]{1,0:T(8,128)(2,1)} %add_convert_fusion.19), channel_id=1, source_target_pairs={{0,8},{8,0},{16,24},{24,16},{1,9},{9,1},{17,25},{25,17},{2,10},{10... | collective-permute-start | bytes 147464 | tf_op jit(solution)/shard_map/ppermute | solution.py:1062
  361.0 6.6 %collective-permute-start.47 = (bf16[64,384]{1,0:T(8,128)(2,1)S(1)}, bf16[64,384]{1,0:T(8,128)(2,1)S(1)}, u32[]{:S(2)}, u32[]{:S(2)}) collective-permute-start(bf16[64,384]{1,0:T(8,128)(2,1)S(1)} %copy-done.30), channel_id=1, source_target_pairs={{0,16},{8,24},{16,0},{24,8},{1,17},{9,25},{17,1},{25,9},{2,18},{10... | collective-permute-start | bytes 147464 | tf_op jit(solution)/shard_map/ppermute | solution.py:1062
  369.6 7.5 %collective-permute-start.52 = (bf16[1152,384]{1,0:T(8,128)(2,1)S(1)}, bf16[1152,384]{1,0:T(8,128)(2,1)S(1)}, u32[]{:S(2)}, u32[]{:S(2)}) collective-permute-start(bf16[1152,384]{1,0:T(8,128)(2,1)S(1)} %maximum_select_fusion.2), channel_id=1, source_target_pairs={{0,2},{2,0},{4,6},{6,4},{1,3},{3,1},{5,7},{7,5},{8,10},{10,8},{12,... | collective-permute-start | bytes 2654216 | tf_op jit(solution)/shard_map/ppermute | solution.py:1062
  369.6 7.3 %collective-permute-start.51 = (bf16[256,384]{1,0:T(8,128)(2,1)S(1)}, bf16[256,384]{1,0:T(8,128)(2,1)S(1)}, u32[]{:S(2)}, u32[]{:S(2)}) collective-permute-start(bf16[256,384]{1,0:T(8,128)(2,1)S(1)} %maximum_select_fusion.13), channel_id=1, source_target_pairs={{0,4},{2,6},{4,0},{6,2},{1,5},{3,7},{5,1},{7,3},{8,12},{10,14},{12... | collective-permute-start | bytes 589832 | tf_op jit(solution)/shard_map/ppermute | solution.py:1062
  (49 other events, 254.3 us)
Sparse Core Ops, SparseCore 0:
  226.6 62.0 reduce-scatter.1
  291.3 45.9 all-gather.1
where the time goes:
time: 402 us; the launch traced here: 394 us
  Pallas kernels  229 us (57%)
  starting transfers between devices  58.5 us (15%)
  waiting for transfers between devices  41 us (10%)
  other arithmetic  30.3 us (8%)
  local copies, waits for them, and re-layouts  20.3 us (5%)
  between operations  15.6 us (4%)
    ppermute x55, starting transfers between devices, cross_to(): return lax.ppermute(value, axis, [(i, i ^ flip) for i in range(count)])  58.5 us
    pallas_call x3, Pallas kernels, back_pass(): pl.pallas_call(functools.partial(back_kernel, pairs, at, more), grid_spec...  51.7 us
    ppermute x55, waiting for transfers between devices, cross_to(): return lax.ppermute(value, axis, [(i, i ^ flip) for i in range(count)])  41 us
    pallas_call x1, Pallas kernels, middle_pass(): pl.pallas_call(functools.partial(middle_kernel, pairs, tile), grid=(rows...  34.1 us
    pallas_call x1, Pallas kernels, feed_pass(): pl.pallas_call(functools.partial(feed_kernel, tile), grid=(2,), in_specs=...  31.5 us
    pallas_call x2, Pallas kernels, query_pass(): pl.pallas_call(functools.partial(query_kernel, pairs, len(weights)), grid...  30.6 us
    pallas_call x2, Pallas kernels, key_pass(): pl.pallas_call(functools.partial(keys_kernel, pairs, len(weights), len(ea...  20.9 us
    pallas_call x2, Pallas kernels, tokens_pass(): pl.pallas_call(kernel, grid=(blocks,), in_specs=[scalars] + [cut(width)]...  18.5 us
  transfers between devices with their start and end apart: 57, of which 18 were waited for; matrix products, arithmetic and copies ran while one was open for 9% of the time, Pallas kernels for 50%

commit v1 on v0

--- a/solution.py
+++ b/solution.py
@@ -1387,8 +1387,8 @@
             (up_sum,) = rest
             up_sum = lax.all_gather(up_sum, everyone, axis=0, tiled=True)
     order = order + 0 * near[0]
-    tokens_args = (tokens, grad_resid, gain_one_row, qkv_own, qkv_oth, grads[0] + grads[1], 256)
-    blocks = rows // 256
+    tokens_args = (tokens, grad_resid, gain_one_row, qkv_own, qkv_oth, grads[0] + grads[1], 384)
+    blocks = rows // 384
     early = blocks // 2
     grad_tokens = tokens_pass(order, *tokens_args, 0, early)
     tail = ["qkv1", "qkv0"]

time: 402 us -> 402 us (level)
  transfers between devices with their start and end apart: 57 -> 57, of which waited for: 18 -> 19; matrix products, arithmetic and copies ran while one was open for 9% -> 9% of each run, Pallas kernels for 50% -> 50%
where the time goes in v1:
time: 402 us; the launch traced here: 394 us
  Pallas kernels  229 us (57%)
  starting transfers between devices  58.1 us (14%)
  waiting for transfers between devices  40.4 us (10%)
  other arithmetic  30.3 us (8%)
  local copies, waits for them, and re-layouts  20.3 us (5%)
  between operations  15.6 us (4%)
    ppermute x55, starting transfers between devices, cross_to(): return lax.ppermute(value, axis, [(i, i ^ flip) for i in range(count)])  58 us
    pallas_call x3, Pallas kernels, back_pass(): pl.pallas_call(functools.partial(back_kernel, pairs, at, more), grid_spec...  51.7 us
    ppermute x55, waiting for transfers between devices, cross_to(): return lax.ppermute(value, axis, [(i, i ^ flip) for i in range(count)])  40.4 us
    pallas_call x1, Pallas kernels, middle_pass(): pl.pallas_call(functools.partial(middle_kernel, pairs, tile), grid=(rows...  34.1 us
    pallas_call x1, Pallas kernels, feed_pass(): pl.pallas_call(functools.partial(feed_kernel, tile), grid=(2,), in_specs=...  31.5 us
    pallas_call x2, Pallas kernels, query_pass(): pl.pallas_call(functools.partial(query_kernel, pairs, len(weights)), grid...  30.6 us
    pallas_call x2, Pallas kernels, key_pass(): pl.pallas_call(functools.partial(keys_kernel, pairs, len(weights), len(ea...  20.9 us
    pallas_call x2, Pallas kernels, tokens_pass(): pl.pallas_call(kernel, grid=(blocks,), in_specs=[scalars] + [cut(width)]...  18.9 us
  transfers between devices with their start and end apart: 57, of which 19 were waited for; matrix products, arithmetic and copies ran while one was open for 9% of the time, Pallas kernels for 50%

profile of v1, /device:TPU:0, one launch (start us, length us, event | category | flops | bytes accessed | tf_op | source)
XLA Modules:
  0.0 393.9 jit_solution(11320437765800370893)
XLA Ops:
  8.6 3.0 collective-permute-start
  12.9 5.2 %norm_one.1 = (bf16[1536,768]{1,0:T(8,128)(2,1)}, bf16[768,1536]{1,0:T(8,128)(2,1)}) custom-call(bf16[1536,768]{1,0:T(8,128)(2,1)} %refs_1_.1, f32[1,768]{1,0:T(1,128)} %reshape.68.gain.refs_3_), custom_call_target="tpu_custom_call" | custom-call | bytes 18000000 | tf_op jit(solution)/shard_map/norm_one/pallas_call | solution.py:140
  18.8 10.4 %key_pass.2 = (bf16[384,1536]{1,0:T(8,128)(2,1)}, bf16[1536,384]{1,0:T(8,128)(2,1)}, bf16[384,1536]{1,0:T(8,128)(2,1)}, bf16[1536,768]{1,0:T(8,128)(2,1)}, bf16[...) custom-call(s32[10]{0:T(128)} %stack.81.order.refs_0_, ...), custom_call_target="tpu_custom_call" | custom-call | bytes 36000000 | tf_op jit(solution)/shard_map/key_pass/pallas_call | solution.py:228
  31.3 1.9 constant_dynamic-slice_fusion.2
  33.2 2.3 collective-permute-done.1.f
  35.6 1.8 collective-permute-start.3
  38.9 10.5 %key_pass.3 = (bf16[384,1536]{1,0:T(8,128)(2,1)}, bf16[1536,384]{1,0:T(8,128)(2,1)}, bf16[384,1536]{1,0:T(8,128)(2,1)}, bf16[1536,768]{1,0:T(8,128)(2,1)}, bf16[...) custom-call(s32[10]{0:T(128)} %stack.81.order.refs_0_, ...), custom_call_target="tpu_custom_call" | custom-call | bytes 36000000 | tf_op jit(solution)/shard_map/key_pass/pallas_call | solution.py:228
  49.4 2.7 collective-permute-done.3.refs_0_
  52.1 1.8 collective-permute-start.5
  55.5 15.2 %query_pass.2 = (bf16[384,1536]{1,0:T(8,128)(2,1)}, bf16[1536,768]{1,0:T(8,128)(2,1)}, bf16[768,1536]{1,0:T(8,128)(2,1)}, bf16[1536,768]{1,0:T(8,128)(2,1)}, bf1...) custom-call(s32[10]{0:T(128)} %stack.81.order.refs_0_, bf16[1536,768]{1,0:T(8,128)(2,1)} %get-tuple-element.177.h, ...), custom_call_target="tpu_custom_call" | custom-call | bytes 54000000 | tf_op jit(solution)/shard_map/query_pass/pallas_call | solution.py:320
  75.3 1.8 collective-permute-start.11
  77.1 1.6 collective-permute-start.10
  79.4 15.4 %query_pass.3 = (bf16[384,1536]{1,0:T(8,128)(2,1)}, bf16[1536,768]{1,0:T(8,128)(2,1)}, bf16[768,1536]{1,0:T(8,128)(2,1)}, bf16[1536,768]{1,0:T(8,128)(2,1)}, bf1...) custom-call(s32[10]{0:T(128)} %stack.81.order.refs_0_, bf16[1536,768]{1,0:T(8,128)(2,1)} %get-tuple-element.177.h, ...), custom_call_target="tpu_custom_call" | custom-call | bytes 54000000 | tf_op jit(solution)/shard_map/query_pass/pallas_call | solution.py:320
  94.9 2.0 select_add_fusion.1.refs_4_.refs_30_
  97.5 1.7 collective-permute-done.13.refs_10_.refs_7_.refs_14_
  100.1 13.0 %front_pass.1 = (bf16[1536,768]{1,0:T(8,128)(2,1)}, bf16[768,1536]{1,0:T(8,128)(2,1)}, bf16[1536,768]{1,0:T(8,128)(2,1)}, bf16[1536,768]{1,0:T(8,128)(2,1)}, bf1...) custom-call(s32[10]{0:T(128)} %stack.81.order.refs_0_, bf16[1536,768]{1,0:T(8,128)(2,1)} %refs_1_.1, ...), custom_call_target="tpu_custom_call" | custom-call | bytes 46800000 | tf_op jit(solution)/shard_map/front_pass/pallas_call | solution.py:440
  113.2 31.5 %feed_pass.1 = (bf16[768,768]{1,0:T(8,128)(2,1)}, bf16[768,768]{1,0:T(8,128)(2,1)}, bf16[768,768]{1,0:T(8,128)(2,1)}, bf16[768,768]{1,0:T(8,128)(2,1)}, bf16[153...) custom-call(s32[10]{0:T(128)} %stack.81.order.refs_0_, bf16[1536,768]{1,0:T(8,128)(2,1)} %get-tuple-element.212.h_any.h, ...), custom_call_target="tpu_custom_call" | custom-call | bytes 115200000 | tf_op jit(solution)/shard_map/feed_pass/pallas_call | solution.py:623
  145.3 2.5 collective-permute-done.16
  147.8 1.7 add_convert_fusion.5
  151.9 34.1 %middle_pass.1 = (bf16[1536,1536]{1,0:T(8,128)(2,1)}, bf16[2,1536,768]{2,1,0:T(8,128)(2,1)}, bf16[1536,768]{1,0:T(8,128)(2,1)}, bf16[1536,768]{1,0:T(8,128)(2,1)...) custom-call(s32[10]{0:T(128)} %stack.81.order.refs_0_, ...), custom_call_target="tpu_custom_call" | custom-call | bytes 126000000 | tf_op jit(solution)/shard_map/middle_pass/pallas_call | solution.py:755
  186.1 4.6 %collective-permute-done.18 = bf16[384,768]{1,0:T(8,128)(2,1)S(1)} collective-permute-done((bf16[384,768]{1,0:T(8,128)(2,1)S(1)}, bf16[384,768]{1,0:T(8,128)(2,1)S(1)}, u32[]{:S(2)}, u32[]{:S(2)}) %collective-permute-start.18) | collective-permute-done | bytes 589856 | tf_op jit(solution)/shard_map/ppermute | solution.py:1062
  192.1 8.1 %up_pass.1 = bf16[768,1536]{1,0:T(8,128)(2,1)} custom-call(s32[1]{0:T(128)} %bitcast.4.core, bf16[768,1536]{1,0:T(8,128)(2,1)} %get-tuple-element.213.turned_any.left, bf16[2,1536,768]{2,1,0:T(8,128)(2,1)} %get-tuple-element.239.right, bf16[768,768]{1,0:T(8,128)(2,1)} %copy-done.15), custom_call_target="tpu_custom_call" | custom-call | bytes 28800000 | tf_op jit(solution)/shard_map/up_pass/pallas_call | solution.py:801
  203.4 7.4 %down_pass.2 = (bf16[768,768]{1,0:T(8,128)(2,1)}, bf16[2,384,384]{2,1,0:T(8,128)(2,1)}) custom-call(s32[1]{0:T(128)} %bitcast.5.core, bf16[1536,1536]{1,0:T(8,128)(2,1)} %get-tuple-element.243.left, bf16[1536,768]{1,0:T(8,128)(2,1)} %right.3, bf16[768,1536]{1,0:T(8,128)(2,1)} %get-tuple-element.244.own_left.oth_left, ...), custom_call_target="tpu_custom_call" | custom-call | bytes 28800000 | tf_op jit(solution)/shard_map/down_pass/pallas_call | solution.py:833
  210.9 2.0 collective-permute-done.22
  215.7 7.5 %down_pass.3 = (bf16[768,768]{1,0:T(8,128)(2,1)}, bf16[2,384,384]{2,1,0:T(8,128)(2,1)}) custom-call(s32[1]{0:T(128)} %bitcast.4.core, bf16[1536,1536]{1,0:T(8,128)(2,1)} %get-tuple-element.243.left, bf16[1536,768]{1,0:T(8,128)(2,1)} %right.3, bf16[768,1536]{1,0:T(8,128)(2,1)} %get-tuple-element.244.own_left.oth_left, ...), custom_call_target="tpu_custom_call" | custom-call | bytes 28800000 | tf_op jit(solution)/shard_map/down_pass/pallas_call | solution.py:833
  226.6 17.2 %back_pass.3 = (bf16[1536,384]{1,0:T(8,128)(2,1)}, bf16[1536,384]{1,0:T(8,128)(2,1)}, bf16[2,384,384]{2,1,0:T(8,128)(2,1)}, bf16[2,384,384]{2,1,0:T(8,128)(2,1)}, bf16[2,128,128]{2,1,0:T(8,128)(2,1)}) custom-call(s32[1]{0:T(128)} %bitcast.4.core, bf16[384,1536]{1,0:T(8,128)(2,1)} %get-tuple-element.256.refs_0_, ...), custom_call_target="tpu_custom_call" | custom-call | bytes 61200000 | tf_op jit(solution)/shard_map/back_pass/pallas_call | solution.py:968
  244.5 16.9 %back_pass.4 = (bf16[1536,384]{1,0:T(8,128)(2,1)}, bf16[1536,384]{1,0:T(8,128)(2,1)}, bf16[2,384,384]{2,1,0:T(8,128)(2,1)}, bf16[2,384,384]{2,1,0:T(8,128)(2,1)}, bf16[2,128,128]{2,1,0:T(8,128)(2,1)}) custom-call(s32[1]{0:T(128)} %bitcast.4.core, bf16[384,1536]{1,0:T(8,128)(2,1)} %get-tuple-element.256.refs_0_, ...), custom_call_target="tpu_custom_call" | custom-call | bytes 61200000 | tf_op jit(solution)/shard_map/back_pass/pallas_call | solution.py:968
  268.4 2.6 collective-permute-start.29
  271.0 17.6 %back_pass.5 = (bf16[1536,384]{1,0:T(8,128)(2,1)}, bf16[1536,384]{1,0:T(8,128)(2,1)}, bf16[2,512,384]{2,1,0:T(8,128)(2,1)}, bf16[2,512,384]{2,1,0:T(8,128)(2,1)}, bf16[2,128,128]{2,1,0:T(8,128)(2,1)}) custom-call(s32[1]{0:T(128)} %bitcast.4.core, bf16[384,1536]{1,0:T(8,128)(2,1)} %get-tuple-element.256.refs_0_, ...), custom_call_target="tpu_custom_call" | custom-call | bytes 61200000 | tf_op jit(solution)/shard_map/back_pass/pallas_call | solution.py:968
  290.6 1.8 collective-permute-done.30
  294.6 2.6 collective-permute-start.33
  297.2 9.4 %tokens_pass.2.refs_13_ = bf16[1536,768]{1,0:T(8,128)(2,1)} custom-call(s32[10]{0:T(128)} %stack.81.order.refs_0_, bf16[1536,768]{1,0:T(8,128)(2,1)} %refs_1_.1, bf16[1536,768]{1,0:T(8,128)(2,1)} %get-tuple-element.245.right_more.refs_2_, f32[1,768]{1,0:T(1,128)} %reshape.68.gain.refs_3_, bf16[3,768,384]{2,1,0:T(8,128)(2,1)} %bitcast.47, ...), custom_call_target="tpu_custom_call" | custom-call | bytes 28800000 | tf_op jit(solution)/shard_map/tokens_pass/pallas_call | solution.py:1037
  307.0 1.7 collective-permute-start.35
  308.7 3.4 collective-permute-start.36
  313.2 9.5 %tokens_pass.3 = bf16[1536,768]{1,0:T(8,128)(2,1)} custom-call(s32[10]{0:T(128)} %stack.81.order.refs_0_, bf16[1536,768]{1,0:T(8,128)(2,1)} %refs_1_.1, bf16[1536,768]{1,0:T(8,128)(2,1)} %get-tuple-element.245.right_more.refs_2_, f32[1,768]{1,0:T(1,128)} %reshape.68.gain.refs_3_, bf16[3,768,384]{2,1,0:T(8,128)(2,1)} %bitcast.48, ...), custom_call_target="tpu_custom_call", output_to_operand_aliasing={{}: (13, {})} | custom-call | bytes 28800000 | tf_op jit(solution)/shard_map/tokens_pass/pallas_call | solution.py:1037
  322.9 6.8 %collective-permute-done.38 = bf16[192,768]{1,0:T(8,128)(2,1)S(1)} collective-permute-done((bf16[192,768]{1,0:T(8,128)(2,1)S(1)}, bf16[192,768]{1,0:T(8,128)(2,1)S(1)}, u32[]{:S(2)}, u32[]{:S(2)}) %collective-permute-start.38) | collective-permute-done | bytes 294944 | tf_op jit(solution)/shard_map/ppermute | solution.py:1062
  329.8 2.5 collective-permute-start.39
  332.4 5.5 %collective-permute-start.40 = (bf16[64,384]{1,0:T(8,128)(2,1)S(1)}, bf16[64,384]{1,0:T(8,128)(2,1)S(1)}, u32[]{:S(2)}, u32[]{:S(2)}) collective-permute-start(bf16[64,384]{1,0:T(8,128)(2,1)S(1)} %get-tuple-element.321), channel_id=1, source_target_pairs={{0,16},{8,24},{16,0},{24,8},{1,17},{9,25},{17,1},{25,9},{2,18},{10... | collective-permute-start | bytes 147464 | tf_op jit(solution)/shard_map/ppermute | solution.py:1062
  339.1 3.8 collective-permute-start.43
  345.6 4.5 %collective-permute-done.43 = bf16[144,384]{1,0:T(8,128)(2,1)S(1)} collective-permute-done((bf16[144,384]{1,0:T(8,128)(2,1)S(1)}, bf16[144,384]{1,0:T(8,128)(2,1)S(1)}, u32[]{:S(2)}, u32[]{:S(2)}) %collective-permute-start.43) | collective-permute-done | bytes 110624 | tf_op jit(solution)/shard_map/ppermute | solution.py:1062
  351.1 2.0 maximum_select_fusion.1
  355.5 2.5 multiply_reduce_fusion
  358.0 2.8 convert_element_type.465
  362.1 1.8 collective-permute-start.48
  363.9 3.3 collective-permute-done.47
  369.6 1.8 collective-permute-start.51
  371.3 4.4 %fusion.1 = f32[1536,768]{1,0:T(8,128)} fusion(bf16[768,768]{1,0:T(8,128)(2,1)} %copy-done.12, bf16[768,768]{1,0:T(8,128)(2,1)S(1)} %maximum_select_fusion.1, pred[]{:T(512)S(6)} %eq.68), kind=kLoop, calls=%fused_computation.5 | loop fusion | flops 11796480 | bytes 7077889 | tf_op jit(solution)/shard_map/convert_element_type | solution.py:1403
  382.7 2.1 convert_bitcast_fusion
  (241 shorter events, 61.8 us)
Async XLA Ops:
  7.2 282.6 %reduce-scatter.2.cloned.1.call-start = ((), (), s32[]{:S(2)}) async-start(), calls=%async_computation.1 | async-start | bytes 2506752 | tf_op jit(solution)/shard_map/reduce_scatter | solution.py:1339
  8.6 26.9 %collective-permute-start = (bf16[3,384,384]{2,1,0:T(8,128)(2,1)S(1)}, bf16[3,384,384]{2,1,0:T(8,128)(2,1)S(1)}, u32[]{:S(2)}, u32[]{:S(2)}) collective-permute-start(bf16[3,384,384]{2,1,0:T(8,128)(2,1)S(1)} %dynamic-slice_bitcast_fusion), channel_id=1, source_target_pairs={{0,1},{1,0},{2,3},{3,2},{4,5},{5,4},{6,7},{7,6},{8,9},{9,8},{10,11... | collective-permute-start | bytes 2654216 | tf_op jit(solution)/shard_map/ppermute | solution.py:1062
  11.7 23.9 %collective-permute-start.1 = (bf16[2,6,64,64]{3,2,1,0:T(8,128)(2,1)S(1)}, bf16[2,6,64,64]{3,2,1,0:T(8,128)(2,1)S(1)}, u32[]{:S(2)}, u32[]{:S(2)}) collective-permute-start(bf16[2,6,64,64]{3,2,1,0:T(8,128)(2,1)S(1)} %pad_maximum_fusion.3.f), channel_id=1, source_target_pairs={{0,1},{1,0},{2,3},{3,2},{4,5},{5,4},{6,7},{7,6},{8,9},{9,8},{10,11... | collective-permute-start | bytes 294920 | tf_op jit(solution)/shard_map/ppermute | solution.py:1062
  35.6 16.5 %collective-permute-start.3 = (bf16[768,384]{1,0:T(8,128)(2,1)}, bf16[768,384]{1,0:T(8,128)(2,1)}, u32[]{:S(2)}, u32[]{:S(2)}) collective-permute-start(bf16[768,384]{1,0:T(8,128)(2,1)} %constant_dynamic-slice_fusion.2), channel_id=1, source_target_pairs={{0,1},{1,0},{2,3},{3,2},{4,5},{5,4},{6,7},{7,6},{8,9},{9,8},{10,11... | collective-permute-start | bytes 1769480 | tf_op jit(solution)/shard_map/ppermute | solution.py:1062
  37.4 36.2 %collective-permute-start.7 = (bf16[480,768]{1,0:T(8,128)(2,1)S(1)}, bf16[480,768]{1,0:T(8,128)(2,1)S(1)}, u32[]{:S(2)}, u32[]{:S(2)}) collective-permute-start(bf16[480,768]{1,0:T(8,128)(2,1)S(1)} %pad_maximum_fusion.2), channel_id=1, source_target_pairs={{0,1},{1,0},{2,3},{3,2},{4,5},{5,4},{6,7},{7,6},{8,9},{9,8},{10,11... | collective-permute-start | bytes 2211848 | tf_op jit(solution)/shard_map/ppermute | solution.py:1062
  52.1 21.5 %collective-permute-start.5 = (bf16[768,384]{1,0:T(8,128)(2,1)}, bf16[768,384]{1,0:T(8,128)(2,1)S(1)}, u32[]{:S(2)}, u32[]{:S(2)}) collective-permute-start(bf16[768,384]{1,0:T(8,128)(2,1)} %collective-permute-done.3.refs_0_), channel_id=1, source_target_pairs={{0,4},{2,6},{4,0},{6,2},{1,5},{3,7},{5,1},{7,3},{8,12},{10,14},{12... | collective-permute-start | bytes 1769480 | tf_op jit(solution)/shard_map/ppermute | solution.py:1062
  53.9 19.7 %collective-permute-start.6 = (bf16[768,384]{1,0:T(8,128)(2,1)}, bf16[768,384]{1,0:T(8,128)(2,1)S(1)}, u32[]{:S(2)}, u32[]{:S(2)}) collective-permute-start(bf16[768,384]{1,0:T(8,128)(2,1)} %collective-permute-done.3.refs_0_), channel_id=1, source_target_pairs={{0,2},{2,0},{4,6},{6,4},{1,3},{3,1},{5,7},{7,5},{8,10},{10,8},{12,... | collective-permute-start | bytes 1769480 | tf_op jit(solution)/shard_map/ppermute | solution.py:1062
  53.9 18.0 %collective-permute-start.4 = (bf16[2,400,128]{2,1,0:T(8,128)(2,1)}, bf16[2,400,128]{2,1,0:T(8,128)(2,1)}, u32[]{:S(2)}, u32[]{:S(2)}) collective-permute-start(bf16[2,400,128]{2,1,0:T(8,128)(2,1)} %get-tuple-element.187), channel_id=1, source_target_pairs={{0,1},{1,0},{2,3},{3,2},{4,5},{5,4},{6,7},{7,6},{8,9},{9,8},{10,11... | collective-permute-start | bytes 614408 | tf_op jit(solution)/shard_map/ppermute | solution.py:1062
  75.3 21.6 %collective-permute-start.11 = (bf16[480,768]{1,0:T(8,128)(2,1)S(1)}, bf16[480,768]{1,0:T(8,128)(2,1)S(1)}, u32[]{:S(2)}, u32[]{:S(2)}) collective-permute-start(bf16[480,768]{1,0:T(8,128)(2,1)S(1)} %collective-permute-done.7.refs_7_.refs_4_.refs_11_), channel_id=1, source_target_pairs={{0,8},{8,0},{16,24},{24,16},{1,9},{9,1},{17,25},{25,17},{2,10},{10... | collective-permute-start | bytes 2211848 | tf_op jit(solution)/shard_map/ppermute | solution.py:1062
  77.1 19.8 %collective-permute-start.12 = (bf16[480,768]{1,0:T(8,128)(2,1)S(1)}, bf16[480,768]{1,0:T(8,128)(2,1)S(1)}, u32[]{:S(2)}, u32[]{:S(2)}) collective-permute-start(bf16[480,768]{1,0:T(8,128)(2,1)S(1)} %collective-permute-done.7.refs_7_.refs_4_.refs_11_), channel_id=1, source_target_pairs={{0,2},{2,0},{4,6},{6,4},{1,3},{3,1},{5,7},{7,5},{8,10},{10,8},{12,... | collective-permute-start | bytes 2211848 | tf_op jit(solution)/shard_map/ppermute | solution.py:1062
  77.1 17.8 %collective-permute-start.10 = (bf16[2,400,128]{2,1,0:T(8,128)(2,1)}, bf16[2,400,128]{2,1,0:T(8,128)(2,1)S(1)}, u32[]{:S(2)}, u32[]{:S(2)}) collective-permute-start(bf16[2,400,128]{2,1,0:T(8,128)(2,1)} %fusion.7), channel_id=1, source_target_pairs={{0,6},{2,4},{4,2},{6,0},{1,7},{3,5},{5,3},{7,1},{8,14},{10,12},{12... | collective-permute-start | bytes 614408 | tf_op jit(solution)/shard_map/ppermute | solution.py:1062
  78.8 16.2 %collective-permute-start.8 = (bf16[2,400,128]{2,1,0:T(8,128)(2,1)}, bf16[2,400,128]{2,1,0:T(8,128)(2,1)}, u32[]{:S(2)}, u32[]{:S(2)}) collective-permute-start(bf16[2,400,128]{2,1,0:T(8,128)(2,1)} %fusion.7), channel_id=1, source_target_pairs={{0,2},{2,0},{4,6},{6,4},{1,3},{3,1},{5,7},{7,5},{8,10},{10,8},{12,... | collective-permute-start | bytes 614408 | tf_op jit(solution)/shard_map/ppermute | solution.py:1062
  78.8 16.2 %collective-permute-start.9 = (bf16[2,400,128]{2,1,0:T(8,128)(2,1)}, bf16[2,400,128]{2,1,0:T(8,128)(2,1)}, u32[]{:S(2)}, u32[]{:S(2)}) collective-permute-start(bf16[2,400,128]{2,1,0:T(8,128)(2,1)} %fusion.7), channel_id=1, source_target_pairs={{0,4},{2,6},{4,0},{6,2},{1,5},{3,7},{5,1},{7,3},{8,12},{10,14},{12... | collective-permute-start | bytes 614408 | tf_op jit(solution)/shard_map/ppermute | solution.py:1062
  97.2 15.9 %collective-permute-start.14 = (bf16[768,384]{1,0:T(8,128)(2,1)S(1)}, bf16[768,384]{1,0:T(8,128)(2,1)}, u32[]{:S(2)}, u32[]{:S(2)}) collective-permute-start(bf16[768,384]{1,0:T(8,128)(2,1)S(1)} %copy-done.19), channel_id=1, source_target_pairs={{0,2},{2,0},{4,6},{6,4},{1,3},{3,1},{5,7},{7,5},{8,10},{10,8},{12,... | collective-permute-start | bytes 1769480 | tf_op jit(solution)/shard_map/ppermute | solution.py:1062
  149.8 40.8 %collective-permute-start.17 = (bf16[768,768]{1,0:T(8,128)(2,1)S(1)}, bf16[768,768]{1,0:T(8,128)(2,1)S(1)}, u32[]{:S(2)}, u32[]{:S(2)}) collective-permute-start(bf16[768,768]{1,0:T(8,128)(2,1)S(1)} %add_convert_fusion), channel_id=1, source_target_pairs={{0,1},{1,0},{2,3},{3,2},{4,5},{5,4},{6,7},{7,6},{8,9},{9,8},{10,11... | collective-permute-start | bytes 3538952 | tf_op jit(solution)/shard_map/ppermute | solution.py:1062
  151.4 39.2 %collective-permute-start.18 = (bf16[384,768]{1,0:T(8,128)(2,1)S(1)}, bf16[384,768]{1,0:T(8,128)(2,1)S(1)}, u32[]{:S(2)}, u32[]{:S(2)}) collective-permute-start(bf16[384,768]{1,0:T(8,128)(2,1)S(1)} %get-tuple-element.232), channel_id=1, source_target_pairs={{0,1},{1,0},{2,3},{3,2},{4,5},{5,4},{6,7},{7,6},{8,9},{9,8},{10,11... | collective-permute-start | bytes 1769480 | tf_op jit(solution)/shard_map/ppermute | solution.py:1062
  190.6 9.6 %collective-permute-start.19 = (bf16[2,400,128]{2,1,0:T(8,128)(2,1)}, bf16[2,400,128]{2,1,0:T(8,128)(2,1)S(1)}, u32[]{:S(2)}, u32[]{:S(2)}) collective-permute-start(bf16[2,400,128]{2,1,0:T(8,128)(2,1)} %get-tuple-element.235), channel_id=1, source_target_pairs={{0,1},{1,0},{2,3},{3,2},{4,5},{5,4},{6,7},{7,6},{8,9},{9,8},{10,11... | collective-permute-start | bytes 614408 | tf_op jit(solution)/shard_map/ppermute | solution.py:1062
  200.3 14.4 %collective-permute-start.23 = (bf16[384,768]{1,0:T(8,128)(2,1)S(1)}, bf16[384,768]{1,0:T(8,128)(2,1)S(1)}, u32[]{:S(2)}, u32[]{:S(2)}) collective-permute-start(bf16[384,768]{1,0:T(8,128)(2,1)S(1)} %get-tuple-element.247), channel_id=1, source_target_pairs={{0,1},{1,0},{2,3},{3,2},{4,5},{5,4},{6,7},{7,6},{8,9},{9,8},{10,11... | collective-permute-start | bytes 1769480 | tf_op jit(solution)/shard_map/ppermute | solution.py:1062
  201.4 9.4 %collective-permute-start.20 = (bf16[2,400,128]{2,1,0:T(8,128)(2,1)S(1)}, bf16[2,400,128]{2,1,0:T(8,128)(2,1)S(1)}, u32[]{:S(2)}, u32[]{:S(2)}) collective-permute-start(bf16[2,400,128]{2,1,0:T(8,128)(2,1)S(1)} %fusion.10), channel_id=1, source_target_pairs={{0,2},{2,0},{4,6},{6,4},{1,3},{3,1},{5,7},{7,5},{8,10},{10,8},{12,... | collective-permute-start | bytes 614408 | tf_op jit(solution)/shard_map/ppermute | solution.py:1062
  201.4 9.4 %collective-permute-start.21 = (bf16[2,400,128]{2,1,0:T(8,128)(2,1)S(1)}, bf16[2,400,128]{2,1,0:T(8,128)(2,1)S(1)}, u32[]{:S(2)}, u32[]{:S(2)}) collective-permute-start(bf16[2,400,128]{2,1,0:T(8,128)(2,1)S(1)} %fusion.10), channel_id=1, source_target_pairs={{0,4},{2,6},{4,0},{6,2},{1,5},{3,7},{5,1},{7,3},{8,12},{10,14},{12... | collective-permute-start | bytes 614408 | tf_op jit(solution)/shard_map/ppermute | solution.py:1062
  202.9 10.0 %collective-permute-start.22 = (bf16[2,400,128]{2,1,0:T(8,128)(2,1)S(1)}, bf16[2,400,128]{2,1,0:T(8,128)(2,1)S(1)}, u32[]{:S(2)}, u32[]{:S(2)}) collective-permute-start(bf16[2,400,128]{2,1,0:T(8,128)(2,1)S(1)} %fusion.10), channel_id=1, source_target_pairs={{0,6},{2,4},{4,2},{6,0},{1,7},{3,5},{5,3},{7,1},{8,14},{10,12},{12... | collective-permute-start | bytes 614408 | tf_op jit(solution)/shard_map/ppermute | solution.py:1062
  215.6 7.6 %collective-permute-start.24 = (bf16[768,768]{1,0:T(8,128)(2,1)}, bf16[768,768]{1,0:T(8,128)(2,1)S(1)}, u32[]{:S(2)}, u32[]{:S(2)}) collective-permute-start(bf16[768,768]{1,0:T(8,128)(2,1)} %get-tuple-element.251), channel_id=1, source_target_pairs={{0,2},{2,0},{4,6},{6,4},{1,3},{3,1},{5,7},{7,5},{8,10},{10,8},{12,... | collective-permute-start | bytes 3538952 | tf_op jit(solution)/shard_map/ppermute | solution.py:1062
  224.9 18.9 %collective-permute-start.25 = (bf16[384,768]{1,0:T(8,128)(2,1)S(1)}, bf16[384,768]{1,0:T(8,128)(2,1)S(1)}, u32[]{:S(2)}, u32[]{:S(2)}) collective-permute-start(bf16[384,768]{1,0:T(8,128)(2,1)S(1)} %get-tuple-element.278), channel_id=1, source_target_pairs={{0,4},{2,6},{4,0},{6,2},{1,5},{3,7},{5,1},{7,3},{8,12},{10,14},{12... | collective-permute-start | bytes 1769480 | tf_op jit(solution)/shard_map/ppermute | solution.py:1062
  226.5 126.6 %all-gather.2.cloned.1.call-start = ((), (), s32[]{:S(2)}) async-start(), calls=%async_computation.2 | async-start | bytes 2506752 | tf_op jit(solution)/shard_map/all_gather | solution.py:1388
  243.9 18.8 %collective-permute-start.26 = (bf16[192,768]{1,0:T(8,128)(2,1)S(1)}, bf16[192,768]{1,0:T(8,128)(2,1)S(1)}, u32[]{:S(2)}, u32[]{:S(2)}) collective-permute-start(bf16[192,768]{1,0:T(8,128)(2,1)S(1)} %get-tuple-element.284), channel_id=1, source_target_pairs={{0,8},{8,0},{16,24},{24,16},{1,9},{9,1},{17,25},{25,17},{2,10},{10... | collective-permute-start | bytes 884744 | tf_op jit(solution)/shard_map/ppermute | solution.py:1062
  267.1 21.8 %collective-permute-start.28 = (bf16[1152,384]{1,0:T(8,128)(2,1)S(1)}, bf16[1152,384]{1,0:T(8,128)(2,1)S(1)}, u32[]{:S(2)}, u32[]{:S(2)}) collective-permute-start(bf16[1152,384]{1,0:T(8,128)(2,1)S(1)} %get-tuple-element.343), channel_id=1, source_target_pairs={{0,1},{1,0},{2,3},{3,2},{4,5},{5,4},{6,7},{7,6},{8,9},{9,8},{10,11... | collective-permute-start | bytes 2654216 | tf_op jit(solution)/shard_map/ppermute | solution.py:1062
  268.4 20.2 %collective-permute-start.29 = (bf16[96,768]{1,0:T(8,128)(2,1)S(1)}, bf16[96,768]{1,0:T(8,128)(2,1)S(1)}, u32[]{:S(2)}, u32[]{:S(2)}) collective-permute-start(bf16[96,768]{1,0:T(8,128)(2,1)S(1)} %get-tuple-element.296), channel_id=1, source_target_pairs={{0,16},{8,24},{16,0},{24,8},{1,17},{9,25},{17,1},{25,9},{2,18},{10... | collective-permute-start | bytes 442376 | tf_op jit(solution)/shard_map/ppermute | solution.py:1062
  289.9 16.8 %collective-permute-start.32 = (bf16[576,384]{1,0:T(8,128)(2,1)}, bf16[576,384]{1,0:T(8,128)(2,1)S(1)}, u32[]{:S(2)}, u32[]{:S(2)}) collective-permute-start(bf16[576,384]{1,0:T(8,128)(2,1)} %get-tuple-element.301), channel_id=1, source_target_pairs={{0,4},{2,6},{4,0},{6,2},{1,5},{3,7},{5,1},{7,3},{8,12},{10,14},{12... | collective-permute-start | bytes 1327112 | tf_op jit(solution)/shard_map/ppermute | solution.py:1062
  293.3 13.5 %collective-permute-start.31 = (bf16[512,384]{1,0:T(8,128)(2,1)}, bf16[512,384]{1,0:T(8,128)(2,1)S(1)}, u32[]{:S(2)}, u32[]{:S(2)}) collective-permute-start(bf16[512,384]{1,0:T(8,128)(2,1)} %get-tuple-element.351), channel_id=1, source_target_pairs={{0,1},{1,0},{2,3},{3,2},{4,5},{5,4},{6,7},{7,6},{8,9},{9,8},{10,11... | collective-permute-start | bytes 1179656 | tf_op jit(solution)/shard_map/ppermute | solution.py:1062
  294.6 12.0 %collective-permute-start.33 = (bf16[96,768]{1,0:T(8,128)(2,1)S(1)}, bf16[96,768]{1,0:T(8,128)(2,1)S(1)}, u32[]{:S(2)}, u32[]{:S(2)}) collective-permute-start(bf16[96,768]{1,0:T(8,128)(2,1)S(1)} %add_convert_fusion.11), channel_id=1, source_target_pairs={{0,16},{8,24},{16,0},{24,8},{1,17},{9,25},{17,1},{25,9},{2,18},{10... | collective-permute-start | bytes 442376 | tf_op jit(solution)/shard_map/ppermute | solution.py:1062
  307.0 15.7 %collective-permute-start.35 = (bf16[144,384]{1,0:T(8,128)(2,1)S(1)}, bf16[144,384]{1,0:T(8,128)(2,1)S(1)}, u32[]{:S(2)}, u32[]{:S(2)}) collective-permute-start(bf16[144,384]{1,0:T(8,128)(2,1)S(1)} %get-tuple-element.312), channel_id=1, source_target_pairs={{0,8},{8,0},{16,24},{24,16},{1,9},{9,1},{17,25},{25,17},{2,10},{10... | collective-permute-start | bytes 331784 | tf_op jit(solution)/shard_map/ppermute | solution.py:1062
  308.7 14.0 %collective-permute-start.36 = (bf16[144,384]{1,0:T(8,128)(2,1)S(1)}, bf16[144,384]{1,0:T(8,128)(2,1)S(1)}, u32[]{:S(2)}, u32[]{:S(2)}) collective-permute-start(bf16[144,384]{1,0:T(8,128)(2,1)S(1)} %get-tuple-element.313), channel_id=1, source_target_pairs={{0,16},{8,24},{16,0},{24,8},{1,17},{9,25},{17,1},{25,9},{2,18},{10... | collective-permute-start | bytes 331784 | tf_op jit(solution)/shard_map/ppermute | solution.py:1062
  312.1 10.6 %collective-permute-start.37 = (bf16[144,384]{1,0:T(8,128)(2,1)S(1)}, bf16[144,384]{1,0:T(8,128)(2,1)S(1)}, u32[]{:S(2)}, u32[]{:S(2)}) collective-permute-start(bf16[144,384]{1,0:T(8,128)(2,1)S(1)} %get-tuple-element.314), channel_id=1, source_target_pairs={{0,24},{8,16},{16,8},{24,0},{1,25},{9,17},{17,9},{25,1},{2,26},{10... | collective-permute-start | bytes 331784 | tf_op jit(solution)/shard_map/ppermute | solution.py:1062
  312.1 17.5 %collective-permute-start.38 = (bf16[192,768]{1,0:T(8,128)(2,1)S(1)}, bf16[192,768]{1,0:T(8,128)(2,1)S(1)}, u32[]{:S(2)}, u32[]{:S(2)}) collective-permute-start(bf16[192,768]{1,0:T(8,128)(2,1)S(1)} %maximum_select_fusion.10), channel_id=1, source_target_pairs={{0,8},{8,0},{16,24},{24,16},{1,9},{9,1},{17,25},{25,17},{2,10},{10... | collective-permute-start | bytes 884744 | tf_op jit(solution)/shard_map/ppermute | solution.py:1062
  312.7 10.1 %collective-permute-start.34 = (bf16[256,384]{1,0:T(8,128)(2,1)S(1)}, bf16[256,384]{1,0:T(8,128)(2,1)S(1)}, u32[]{:S(2)}, u32[]{:S(2)}) collective-permute-start(bf16[256,384]{1,0:T(8,128)(2,1)S(1)} %get-tuple-element.310), channel_id=1, source_target_pairs={{0,4},{2,6},{4,0},{6,2},{1,5},{3,7},{5,1},{7,3},{8,12},{10,14},{12... | collective-permute-start | bytes 589832 | tf_op jit(solution)/shard_map/ppermute | solution.py:1062
  329.8 9.3 %collective-permute-start.39 = (bf16[64,384]{1,0:T(8,128)(2,1)S(1)}, bf16[64,384]{1,0:T(8,128)(2,1)S(1)}, u32[]{:S(2)}, u32[]{:S(2)}) collective-permute-start(bf16[64,384]{1,0:T(8,128)(2,1)S(1)} %get-tuple-element.320), channel_id=1, source_target_pairs={{0,8},{8,0},{16,24},{24,16},{1,9},{9,1},{17,25},{25,17},{2,10},{10... | collective-permute-start | bytes 147464 | tf_op jit(solution)/shard_map/ppermute | solution.py:1062
  332.4 10.6 %collective-permute-start.40 = (bf16[64,384]{1,0:T(8,128)(2,1)S(1)}, bf16[64,384]{1,0:T(8,128)(2,1)S(1)}, u32[]{:S(2)}, u32[]{:S(2)}) collective-permute-start(bf16[64,384]{1,0:T(8,128)(2,1)S(1)} %get-tuple-element.321), channel_id=1, source_target_pairs={{0,16},{8,24},{16,0},{24,8},{1,17},{9,25},{17,1},{25,9},{2,18},{10... | collective-permute-start | bytes 147464 | tf_op jit(solution)/shard_map/ppermute | solution.py:1062
  337.9 6.6 %collective-permute-start.41 = (bf16[64,384]{1,0:T(8,128)(2,1)S(1)}, bf16[64,384]{1,0:T(8,128)(2,1)S(1)}, u32[]{:S(2)}, u32[]{:S(2)}) collective-permute-start(bf16[64,384]{1,0:T(8,128)(2,1)S(1)} %get-tuple-element.322), channel_id=1, source_target_pairs={{0,24},{8,16},{16,8},{24,0},{1,25},{9,17},{17,9},{25,1},{2,26},{10... | collective-permute-start | bytes 147464 | tf_op jit(solution)/shard_map/ppermute | solution.py:1062
  337.9 13.2 %collective-permute-start.45 = (bf16[384,768]{1,0:T(8,128)(2,1)S(1)}, bf16[384,768]{1,0:T(8,128)(2,1)}, u32[]{:S(2)}, u32[]{:S(2)}) collective-permute-start(bf16[384,768]{1,0:T(8,128)(2,1)S(1)} %maximum_select_fusion.3), channel_id=1, source_target_pairs={{0,4},{2,6},{4,0},{6,2},{1,5},{3,7},{5,1},{7,3},{8,12},{10,14},{12... | collective-permute-start | bytes 1769480 | tf_op jit(solution)/shard_map/ppermute | solution.py:1062
  338.6 7.0 %collective-permute-start.42 = (bf16[144,384]{1,0:T(8,128)(2,1)S(1)}, bf16[144,384]{1,0:T(8,128)(2,1)S(1)}, u32[]{:S(2)}, u32[]{:S(2)}) collective-permute-start(bf16[144,384]{1,0:T(8,128)(2,1)S(1)} %add_convert_fusion.14), channel_id=1, source_target_pairs={{0,8},{8,0},{16,24},{24,16},{1,9},{9,1},{17,25},{25,17},{2,10},{10... | collective-permute-start | bytes 331784 | tf_op jit(solution)/shard_map/ppermute | solution.py:1062
  339.1 11.0 %collective-permute-start.43 = (bf16[144,384]{1,0:T(8,128)(2,1)S(1)}, bf16[144,384]{1,0:T(8,128)(2,1)S(1)}, u32[]{:S(2)}, u32[]{:S(2)}) collective-permute-start(bf16[144,384]{1,0:T(8,128)(2,1)S(1)} %add_convert_fusion.14), channel_id=1, source_target_pairs={{0,16},{8,24},{16,0},{24,8},{1,17},{9,25},{17,1},{25,9},{2,18},{10... | collective-permute-start | bytes 331784 | tf_op jit(solution)/shard_map/ppermute | solution.py:1062
  343.0 7.1 %collective-permute-start.44 = (bf16[144,384]{1,0:T(8,128)(2,1)S(1)}, bf16[144,384]{1,0:T(8,128)(2,1)S(1)}, u32[]{:S(2)}, u32[]{:S(2)}) collective-permute-start(bf16[144,384]{1,0:T(8,128)(2,1)S(1)} %add_convert_fusion.14), channel_id=1, source_target_pairs={{0,24},{8,16},{16,8},{24,0},{1,25},{9,17},{17,9},{25,1},{2,26},{10... | collective-permute-start | bytes 331784 | tf_op jit(solution)/shard_map/ppermute | solution.py:1062
  353.2 15.4 %collective-permute-start.50 = (bf16[768,768]{1,0:T(8,128)(2,1)S(1)}, bf16[768,768]{1,0:T(8,128)(2,1)S(1)}, u32[]{:S(2)}, u32[]{:S(2)}) collective-permute-start(bf16[768,768]{1,0:T(8,128)(2,1)S(1)} %maximum_select_fusion.1), channel_id=1, source_target_pairs={{0,2},{2,0},{4,6},{6,4},{1,3},{3,1},{5,7},{7,5},{8,10},{10,8},{12,... | collective-permute-start | bytes 3538952 | tf_op jit(solution)/shard_map/ppermute | solution.py:1062
  353.2 14.9 %collective-permute-start.49 = (bf16[576,384]{1,0:T(8,128)(2,1)}, bf16[576,384]{1,0:T(8,128)(2,1)S(1)}, u32[]{:S(2)}, u32[]{:S(2)}) collective-permute-start(bf16[576,384]{1,0:T(8,128)(2,1)} %maximum_select_fusion.8), channel_id=1, source_target_pairs={{0,4},{2,6},{4,0},{6,2},{1,5},{3,7},{5,1},{7,3},{8,12},{10,14},{12... | collective-permute-start | bytes 1327112 | tf_op jit(solution)/shard_map/ppermute | solution.py:1062
  354.1 9.8 %collective-permute-start.46 = (bf16[64,384]{1,0:T(8,128)(2,1)}, bf16[64,384]{1,0:T(8,128)(2,1)S(1)}, u32[]{:S(2)}, u32[]{:S(2)}) collective-permute-start(bf16[64,384]{1,0:T(8,128)(2,1)} %add_convert_fusion.19), channel_id=1, source_target_pairs={{0,8},{8,0},{16,24},{24,16},{1,9},{9,1},{17,25},{25,17},{2,10},{10... | collective-permute-start | bytes 147464 | tf_op jit(solution)/shard_map/ppermute | solution.py:1062
  360.8 6.4 %collective-permute-start.47 = (bf16[64,384]{1,0:T(8,128)(2,1)S(1)}, bf16[64,384]{1,0:T(8,128)(2,1)S(1)}, u32[]{:S(2)}, u32[]{:S(2)}) collective-permute-start(bf16[64,384]{1,0:T(8,128)(2,1)S(1)} %copy-done.30), channel_id=1, source_target_pairs={{0,16},{8,24},{16,0},{24,8},{1,17},{9,25},{17,1},{25,9},{2,18},{10... | collective-permute-start | bytes 147464 | tf_op jit(solution)/shard_map/ppermute | solution.py:1062
  369.5 7.5 %collective-permute-start.52 = (bf16[1152,384]{1,0:T(8,128)(2,1)S(1)}, bf16[1152,384]{1,0:T(8,128)(2,1)S(1)}, u32[]{:S(2)}, u32[]{:S(2)}) collective-permute-start(bf16[1152,384]{1,0:T(8,128)(2,1)S(1)} %maximum_select_fusion.2), channel_id=1, source_target_pairs={{0,2},{2,0},{4,6},{6,4},{1,3},{3,1},{5,7},{7,5},{8,10},{10,8},{12,... | collective-permute-start | bytes 2654216 | tf_op jit(solution)/shard_map/ppermute | solution.py:1062
  369.6 7.3 %collective-permute-start.51 = (bf16[256,384]{1,0:T(8,128)(2,1)S(1)}, bf16[256,384]{1,0:T(8,128)(2,1)S(1)}, u32[]{:S(2)}, u32[]{:S(2)}) collective-permute-start(bf16[256,384]{1,0:T(8,128)(2,1)S(1)} %maximum_select_fusion.13), channel_id=1, source_target_pairs={{0,4},{2,6},{4,0},{6,2},{1,5},{3,7},{5,1},{7,3},{8,12},{10,14},{12... | collective-permute-start | bytes 589832 | tf_op jit(solution)/shard_map/ppermute | solution.py:1062
  (49 other events, 252.7 us)
Sparse Core Ops, SparseCore 0:
  226.6 62.0 reduce-scatter.1
  291.3 45.9 all-gather.1
